TPU v7x, 256 devices: a whole 4x4x8 slice. The times are simulated.
256 devices in a mesh: dp: 16 (over z, x_hi), shard: 16 (over x_lo, y, core).
Axes of the slice: x: 4 (x_hi: 2, x_lo: 2; x = x_hi * 2 + x_lo), y: 4, z: 8, core: 2. Of those that a mesh axis runs over, the one named last changes fastest.
Arguments:
- frames: bfloat16 [4096, 40, 1536], P(('dp', 'shard')), may hold values from -6 to 6
- slot_dest: int32 [4096], P(('dp', 'shard')), may hold values from 0 to 15, as said below
- recv_length: int32 [4096], P(('dp', 'shard')), may hold values from 8 to 40, as said below
- recv_offset: int32 [4096], P(('dp', 'shard')), may hold values from 0 to 383, as said below
- gain1: float32 [1536], replicated, may hold values from 0.5 to 1.5
- w_in: bfloat16 [1536, 3072], P('shard'), may hold values from -0.15625 to 0.15625
- w_depth: float32 [31, 1536], replicated, may hold values from -1 to 1
- gain2: float32 [1536], replicated, may hold values from 0.5 to 1.5
- cotangent: bfloat16 [98304, 1536], P(('dp', 'shard')), may hold values from -6 to 6
Outputs:
- output: bfloat16 [98304, 1536], P(('dp', 'shard'))
- grad_input: bfloat16 [98304, 1536], P(('dp', 'shard'))
- grad_w_in: float32 [1536, 3072], P('shard')
- grad_depth: float32 [31, 1536], replicated
- grad_gain1: float32 [1536], replicated
- grad_gain2: float32 [1536], replicated
Inputs may be any that keep to these rules, and one draw needn't show every extreme that they name: Within each device's block, slot_dest is a permutation of the dp indices: every device holds one utterance for each device of its dp group. recv_length entry s of device (p, g) is the length of the utterance that device (s, g) holds for p; the lengths in each device's block sum to 384, and each block has one of exactly 40. In each device's block the intervals [recv_offset, recv_offset + recv_length) tile the rows 0 to 383 without gaps or intersections.
All inputs are finite; a program needn't handle non-finite values.
Results may differ from a plain program's by a relative error of at most 0.012.
Values may be sent and summed in bfloat16 or wider, within the bound.
A program may use at most 128 MiB of HBM per device.

v0:
```python
import jax
import jax.numpy as jnp
from jax import lax
from jax.sharding import PartitionSpec as P

EPSILON = 1e-05


def gather_frames(pool, bases, lengths, offsets, frame_count, slot_len):
    rows_here = jnp.arange(frame_count, dtype=jnp.int32)[:, None]
    member = ((rows_here >= offsets[None, :]) & (rows_here < (offsets + lengths)[None, :])).astype(
        jnp.int32
    )
    sources = jnp.arange(lengths.shape[0], dtype=jnp.int32)[None, :]
    owner = jnp.sum(member * sources, axis=1)
    within = jnp.sum(member * (rows_here - offsets[None, :]), axis=1)
    base_row = jnp.sum(member * bases[None, :], axis=1)
    picked = jnp.take(pool, base_row * slot_len + within, axis=0)
    return (picked, owner)


def normalize(values):
    center = values - jnp.mean(values, axis=1, keepdims=True)
    inverse = lax.rsqrt(jnp.mean(center * center, axis=1, keepdims=True) + EPSILON)
    return (center * inverse, inverse)


def normalize_back(grad_unit, unit, inverse):
    first = jnp.mean(grad_unit, axis=1, keepdims=True)
    second = jnp.mean(grad_unit * unit, axis=1, keepdims=True)
    return inverse * (grad_unit - first - unit * second)


def depth_forward(values, segment, kernel):
    count = values.shape[0]
    reach = (kernel.shape[0] - 1) // 2
    padded = jnp.pad(values, ((reach, reach), (0, 0)))
    labels = jnp.pad(segment, (reach, reach), constant_values=-1)
    total = jnp.zeros_like(values)
    for tap_index in range(kernel.shape[0]):
        same = (labels[tap_index : tap_index + count] == segment)[:, None]
        total = (
            total + jnp.where(same, padded[tap_index : tap_index + count], 0.0) * kernel[tap_index]
        )
    return total


def depth_backward(grads, segment, kernel):
    count = grads.shape[0]
    reach = (kernel.shape[0] - 1) // 2
    padded = jnp.pad(grads, ((reach, reach), (0, 0)))
    labels = jnp.pad(segment, (reach, reach), constant_values=-1)
    total = jnp.zeros_like(grads)
    for tap_index in range(kernel.shape[0]):
        begin = 2 * reach - tap_index
        same = (labels[begin : begin + count] == segment)[:, None]
        total = total + jnp.where(same, padded[begin : begin + count], 0.0) * kernel[tap_index]
    return total


def depth_weight_grad(grads, values, segment, taps_count):
    count = values.shape[0]
    reach = (taps_count - 1) // 2
    padded = jnp.pad(values, ((reach, reach), (0, 0)))
    labels = jnp.pad(segment, (reach, reach), constant_values=-1)
    collected = []
    for tap_index in range(taps_count):
        same = (labels[tap_index : tap_index + count] == segment)[:, None]
        collected.append(
            jnp.sum(jnp.where(same, padded[tap_index : tap_index + count], 0.0) * grads, axis=0)
        )
    return jnp.stack(collected, axis=0)


def body(frames, slot_dest, recv_length, recv_offset, gain1, w_in, w_depth, gain2, cotangent):
    peers = lax.axis_size("dp")
    devices = peers * lax.axis_size("shard")
    indices = jnp.arange(peers, dtype=jnp.int32)
    chosen = (slot_dest[None, :] == indices[:, None]).astype(jnp.int32)
    source_slot = jnp.sum(chosen * indices[None, :], axis=1)
    outgoing = jnp.take(frames, source_slot, axis=0)
    arrived = lax.all_to_all(outgoing, "dp", split_axis=0, concat_axis=0, tiled=True)
    frame_count = cotangent.shape[0]
    slot_len = frames.shape[1]
    model_width = frames.shape[2]
    inputs, segment = gather_frames(
        arrived.reshape(peers * slot_len, model_width),
        indices,
        recv_length,
        recv_offset,
        frame_count,
        slot_len,
    )
    unit_in, inverse_in = normalize(inputs.astype(jnp.float32))
    normed = (unit_in * gain1).astype(jnp.bfloat16)
    full_weight = lax.all_gather(w_in, "shard", axis=0, tiled=True)
    projected = jnp.dot(normed, full_weight, preferred_element_type=jnp.float32)
    linear = projected[:, :model_width]
    gating = projected[:, model_width:]
    gate_sig = jax.nn.sigmoid(gating)
    gated = (linear * gate_sig).astype(jnp.bfloat16)
    gated_wide = gated.astype(jnp.float32)
    convolved = depth_forward(gated_wide, segment, w_depth)
    unit_out, inverse_out = normalize(convolved)
    scaled = unit_out * gain2
    sig_out = jax.nn.sigmoid(scaled)
    output = (scaled * sig_out).astype(jnp.bfloat16)
    grad_scaled = cotangent.astype(jnp.float32) * sig_out * (1.0 + scaled * (1.0 - sig_out))
    gain2_part = jnp.sum(grad_scaled * unit_out, axis=0)
    grad_conv = normalize_back(grad_scaled * gain2, unit_out, inverse_out)
    depth_part = depth_weight_grad(grad_conv, gated_wide, segment, w_depth.shape[0])
    grad_gated = depth_backward(grad_conv, segment, w_depth)
    grad_pre = jnp.concatenate(
        [grad_gated * gate_sig, grad_gated * linear * gate_sig * (1.0 - gate_sig)], axis=1
    ).astype(jnp.bfloat16)
    grad_normed = lax.dot_general(
        grad_pre, full_weight, (((1,), (1,)), ((), ())), preferred_element_type=jnp.float32
    )
    gain1_part = jnp.sum(grad_normed * unit_in, axis=0)
    grad_input = normalize_back(grad_normed * gain1, unit_in, inverse_in).astype(jnp.bfloat16)
    owned_rows = lax.psum_scatter(
        lax.dot_general(
            normed, grad_pre, (((0,), (0,)), ((), ())), preferred_element_type=jnp.float32
        ),
        "shard",
        scatter_dimension=0,
        tiled=True,
    )
    summed_rows = lax.psum(owned_rows, "dp")
    grad_gain1, grad_gain2, grad_depth = lax.psum(
        (gain1_part, gain2_part, depth_part), ("dp", "shard")
    )
    return (
        output,
        grad_input,
        summed_rows / devices,
        grad_depth / devices,
        grad_gain1 / devices,
        grad_gain2 / devices,
    )


def solution(mesh):
    in_specs = (
        P(("dp", "shard"), None, None),
        P(("dp", "shard")),
        P(("dp", "shard")),
        P(("dp", "shard")),
        P(),
        P("shard", None),
        P(),
        P(),
        P(("dp", "shard"), None),
    )
    out_specs = (
        P(("dp", "shard"), None),
        P(("dp", "shard"), None),
        P("shard", None),
        P(),
        P(),
        P(),
    )
    return jax.shard_map(body, mesh=mesh, in_specs=in_specs, out_specs=out_specs, check_vma=False)
```

profile of v0, /device:TPU:6, one launch (start us, length us, event | category | flops | bytes accessed | tf_op | source)
XLA Modules:
  0.0 744.7 jit_solution(2135444435885315029)
XLA Ops:
  8.7 2.0 gather_fusion
  10.7 3.1 broadcast_select_fusion
  13.8 11.6 %all-to-all-start = ((bf16[16,40,1536]{2,1,0:T(8,128)(2,1)}), bf16[16,40,1536]{2,1,0:T(8,128)(2,1)S(1)}, u32[]{:S(2)}, u32[]{:S(2)}) async-start(bf16[16,40,1536]{2,1,0:T(8,128)(2,1)} %broadcast_select_fusion), calls=%async_computation | async-start | bytes 3932160 | tf_op jit(solution)/shard_map/all_to_all | solution.py:82
  30.0 41.9 %all-to-all-done = bf16[16,40,1536]{2,1,0:T(8,128)(2,1)S(1)} async-done(((bf16[16,40,1536]{2,1,0:T(8,128)(2,1)}), bf16[16,40,1536]{2,1,0:T(8,128)(2,1)S(1)}, u32[]{:S(2)}, u32[]{:S(2)}) %all-to-all-start) | async-done | bytes 1966112 | tf_op jit(solution)/shard_map/all_to_all | solution.py:82
  71.9 2.2 gather_fusion.1
  75.0 17.8 %all-gather.2.cloned.1.call-done = bf16[1536,3072]{1,0:T(8,128)(2,1)} async-done(((bf16[96,3072]{1,0:T(8,128)(2,1)}), bf16[1536,3072]{1,0:T(8,128)(2,1)}) %all-gather.2.cloned.1.call-update) | async-done | bytes 9437200 | tf_op jit(solution)/shard_map/all_gather | solution.py:96
  92.8 6.7 fusion.66
  101.0 18.7 %fusion.68 = (f32[384]{0:T(512)S(1)}, f32[384,1536]{1,0:T(8,128)S(1)}) fusion(f32[1536]{0:T(1024)S(1)} %copy-done.38, pred[384]{0:T(512)(128)(4,1)S(1)} %copy-done.48, f32[1536]{0:T(1024)S(1)} %copy-done.39, pred[384]{0:T(512)(128)(4,1)} %get-tuple-element.88, f32[1536]{0:T(1024)S(1)} %copy-done.10, pred[384]{0:T(512)(128)(4,1)} %get-tuple-element.89, ...), kind=kLoop, calls=%fused_computation.252 | loop fusion | flops 54263424 | bytes 4922112 | tf_op jit(solution)/shard_map/reduce_sum | solution.py:23
  121.0 3.3 multiply_reduce_fusion
  124.5 6.7 multiply_reduce_fusion.1
  131.4 14.8 %multiply_convert_fusion.1 = (bf16[384,1536]{1,0:T(8,128)(2,1)S(1)}, f32[384,1536]{1,0:T(8,128)S(1)}) fusion(f32[384,3072]{1,0:T(8,128)S(1)} %fusion.66, f32[1536]{0:T(1024)S(1)} %copy-done.38, pred[384]{0:T(512)(128)(4,1)S(1)} %copy-done.66, f32[1536]{0:T(1024)S(1)} %copy-done.39, pred[384]{0:T(512)(128)(4,1)S(1)} %copy-done.65, f32[1536]{0:T(1024)S(1)} %copy-done.10, ...), kind=kLoop, calls=%fused_computation.55 | loop fusion | flops 56623104 | bytes 8459520 | tf_op jit(solution)/shard_map/convert
  148.1 9.5 %fusion.57 = f32[1536,3072]{1,0:T(8,128)} fusion(bf16[384,1536]{1,0:T(8,128)(2,1)S(1)} %multiply_convert_fusion, bf16[384,1536]{1,0:T(8,128)(2,1)S(1)} %get-tuple-element.79, f32[1536]{0:T(1024)S(1)} %copy-done.8, f32[384]{0:T(512)S(1)} %add_rsqrt_fusion.1, f32[384]{0:T(512)S(1)} %broadcast_multiply_fusion.9, bf16[384,1536]{1,0:T(8,128)(2,1)S(1)} %gather_fusion.1, ...), kind=kOutput, calls=%fused_computation.154 | convolution fusion | flops 3632136192 | bytes 22422912 | tf_op jit(solution)/shard_map/dot_general | solution.py:122
  157.7 1.3 stack.126
  159.0 1.3 stack.125
  160.3 1.3 stack.124
  161.6 1.3 stack.123
  162.9 1.3 stack.122
  164.2 1.3 stack.121
  165.5 1.3 stack.120
  166.8 1.3 stack.119
  168.1 1.3 stack.118
  169.4 4.1 multiply_reduce_fusion.28
  176.1 5.0 multiply_reduce_fusion.10
  181.8 5.2 multiply_reduce_fusion.19
  187.2 5.0 stack.127
  192.3 10.4 %fusion.11 = (f32[1536]{0:T(1024)S(1)}, f32[384]{0:T(512)S(1)}, f32[384]{0:T(512)S(1)}, f32[384,1536]{1,0:T(8,128)}) fusion(f32[384]{0:T(512)S(1)} %add_rsqrt_fusion.1, f32[384]{0:T(512)S(1)} %broadcast_multiply_fusion.9, bf16[384,1536]{1,0:T(8,128)(2,1)S(1)} %gather_fusion.1, pred[384]{0:T(512)(128)(4,1)} %copy-done.42, f32[1536]{0:T(1024)S(1)} %copy-done.8, ...), kind=kOutput, calls=%fused_computation.15 | convolution fusion | flops 3634492928 | bytes 15354240 | tf_op jit(solution)/shard_map/dot_general | solution.py:116
  202.7 126.1 %all-reduce.3 = (f32[1536]{0:T(1024)S(1)}, f32[1536]{0:T(1024)S(1)}) all-reduce(f32[1536]{0:T(1024)S(1)} %get-tuple-element.39, f32[1536]{0:T(1024)S(1)} %copy-done.41), channel_id=1, replica_groups=mesh['dp'=16,'shard'=16] {'dp','shard'}, use_global_device_ids=true, to_apply=%region_46.47 | all-reduce | flops 3072 | bytes 24576 | tf_op jit(solution)/shard_map/psum | solution.py:130
  330.7 3.6 fusion.10
  334.3 239.4 %all-reduce.9.cloned.1.call-done = f32[31,1536]{1,0:T(8,128)} async-done(((f32[31,1536]{1,0:T(8,128)}), f32[31,1536]{1,0:T(8,128)}) %all-reduce.9.cloned.1.call-update) | async-done | bytes 190480 | tf_op jit(solution)/shard_map/psum | solution.py:130
  573.7 1.6 broadcast_multiply_fusion.1
  575.3 160.5 %all-reduce.7.cloned.1.call-done = f32[96,3072]{1,0:T(8,128)} async-done(((f32[96,3072]{1,0:T(8,128)}), f32[96,3072]{1,0:T(8,128)}) %all-reduce.7.cloned.1.call-update) | async-done | bytes 1179664 | tf_op jit(solution)/shard_map/psum | solution.py:129
  735.8 2.4 broadcast_multiply_fusion
  (247 shorter events, 16.2 us)
Async XLA Ops:
  7.2 85.6 %all-gather.2.cloned.1.call-start = ((), (), s32[]{:S(2)}) async-start(), calls=%async_computation.2 | async-start | bytes 10027008 | tf_op jit(solution)/shard_map/all_gather | solution.py:96
  13.8 11.6 %copy-start.92 = (s32[16]{0:T(128)S(1)}, s32[16]{0:T(128)}, u32[]{:S(2)}) copy-start(s32[16]{0:T(128)} %param.12) | copy-start | bytes 196
  13.8 11.6 %copy-start.93 = (s32[16]{0:T(128)S(1)}, s32[16]{0:T(128)}, u32[]{:S(2)}) copy-start(s32[16]{0:T(128)} %param.11) | copy-start | bytes 196
  13.8 12.4 %copy-start.7 = (f32[31,1536]{1,0:T(8,128)S(1)}, f32[31,1536]{1,0:T(8,128)}, u32[]{:S(2)}) copy-start(f32[31,1536]{1,0:T(8,128)} %param.15) | copy-start | bytes 571396
  13.8 58.1 %all-to-all-start = ((bf16[16,40,1536]{2,1,0:T(8,128)(2,1)}), bf16[16,40,1536]{2,1,0:T(8,128)(2,1)S(1)}, u32[]{:S(2)}, u32[]{:S(2)}) async-start(bf16[16,40,1536]{2,1,0:T(8,128)(2,1)} %broadcast_select_fusion), calls=%async_computation | async-start | bytes 3932160 | tf_op jit(solution)/shard_map/all_to_all | solution.py:82
  25.3 304.8 %reduce-scatter.2.cloned.1.call-start = ((), (), s32[]{:S(2)}) async-start(), calls=%async_computation.3 | async-start | bytes 20054016 | tf_op jit(solution)/shard_map/reduce_scatter | solution.py:121
  26.2 66.7 %copy-start.42 = (pred[384]{0:T(512)(128)(4,1)}, pred[384]{0:T(512)(128)(4,1)S(1)}, u32[]{:S(2)}) copy-start(pred[384]{0:T(512)(128)(4,1)S(1)} %get-tuple-element.116) | copy-start | bytes 1156
  74.1 18.8 %copy-start.8 = (f32[1536]{0:T(1024)S(1)}, f32[1536]{0:T(1024)}, u32[]{:S(2)}) copy-start(f32[1536]{0:T(1024)} %param.13) | copy-start | bytes 18436
  124.4 6.9 copy-start.59
  124.4 6.9 copy-start.61
  124.4 6.9 copy-start.63
  124.4 6.8 copy-start.65
  124.4 6.8 copy-start.66
  124.4 6.8 copy-start.67
  124.5 6.8 copy-start.76
  124.5 6.8 copy-start.78
  124.5 6.8 copy-start.80
  124.5 6.8 copy-start.82
  124.5 6.8 copy-start.84
  124.5 6.8 copy-start.86
  124.5 6.8 copy-start.88
  124.5 6.8 copy-start.90
  131.3 14.9 %copy-start.2 = (f32[384,1536]{1,0:T(8,128)}, f32[384,1536]{1,0:T(8,128)S(1)}, u32[]{:S(2)}) copy-start(f32[384,1536]{1,0:T(8,128)S(1)} %get-tuple-element.78) | copy-start | bytes 7077892
  157.7 416.0 %all-reduce.9.cloned.1.call-start = ((), (), s32[]{:S(2)}) async-start(), calls=%async_computation.5 | async-start | bytes 393216 | tf_op jit(solution)/shard_map/psum | solution.py:130
  169.4 6.6 copy-start.83
  169.4 6.6 copy-start.85
  169.4 6.6 copy-start.87
  169.4 6.6 copy-start.89
  192.3 10.4 %copy-start.41 = (f32[1536]{0:T(1024)S(1)}, f32[1536]{0:T(1024)}, u32[]{:S(2)}) copy-start(f32[1536]{0:T(1024)} %get-tuple-element.6) | copy-start | bytes 18436
  192.3 138.4 %copy-start.44 = (pred[384]{0:T(512)(128)(4,1)S(1)}, pred[384]{0:T(512)(128)(4,1)}, u32[]{:S(2)}) copy-start(pred[384]{0:T(512)(128)(4,1)} %copy-done.42) | copy-start | bytes 1156
  330.1 405.8 %all-reduce.7.cloned.1.call-start = ((), (), s32[]{:S(2)}) async-start(), calls=%async_computation.4 | async-start | bytes 2359296 | tf_op jit(solution)/shard_map/psum | solution.py:129
  330.7 407.5 %copy-start.1 = (bf16[16,40,1536]{2,1,0:T(8,128)(2,1)S(1)}, bf16[16,40,1536]{2,1,0:T(8,128)(2,1)}, u32[]{:S(2)}) copy-start(bf16[16,40,1536]{2,1,0:T(8,128)(2,1)} %param.9) | copy-start | bytes 5898244
  (67 other events, 159.5 us)
Sparse Core Ops, SparseCore 0:
  9.9 82.9 all-gather.1
  157.8 112.9 reduce-scatter.1
  330.2 243.4 all-reduce.8
  576.2 159.5 all-reduce.6
where the time goes:
time: 747 us; the launch traced here: 745 us
  waiting for transfers between devices  461 us (62%)
  blocking collectives  126 us (17%)
  other arithmetic  76.2 us (10%)
  local copies, waits for them, and re-layouts  27.9 us (4%)
  matrix products  26.7 us (4%)
  between operations  15.3 us (2%)
  starting transfers between devices  11.7 us (2%)
    psum x1, waiting for transfers between devices, body(): lax.psum((gain1_part, gain2_part, depth_part), ('dp', 'shard'))  239 us
    psum x1, waiting for transfers between devices, body(): summed_rows = lax.psum(owned_rows, 'dp')  160 us
    psum x1, blocking collectives, body(): lax.psum((gain1_part, gain2_part, depth_part), ('dp', 'shard'))  126 us
    all_to_all x1, waiting for transfers between devices, body(): lax.all_to_all(outgoing, 'dp', split_axis=0, concat_axis=0, tiled=True)  41.9 us
    reduce_sum x4, other arithmetic, depth_weight_grad(): jnp.sum(jnp.where(same, padded[tap_index:tap_index + count], 0.0) * grads...  21 us
    another operation x32, local copies, waits for them, and re-layouts, depth_weight_grad(): return jnp.stack(collected, axis=0)  19.8 us
    reduce_sum x2, other arithmetic, normalize(): center = values - jnp.mean(values, axis=1, keepdims=True)  19.1 us
    all_gather x1, waiting for transfers between devices, body(): full_weight = lax.all_gather(w_in, 'shard', axis=0, tiled=True)  17.8 us
  transfers between devices with their start and end apart: 5, of which 4 were waited for; matrix products, arithmetic and copies ran while one was open for 9% of the time, Pallas kernels for 0%

commit v1 on v0

v1 whole, which is shorter than its diff:
```python
import jax
import jax.numpy as jnp
from jax import lax
from jax.experimental import pallas as pl
from jax.experimental.pallas import tpu as pltpu
from jax.sharding import PartitionSpec as P

EPSILON = 1e-05
MESH = pl.DeviceIdType.MESH
BF = jnp.bfloat16
F32 = jnp.float32

N_DP = 16
N_SHARD = 16
SMALL_ROWS = 40
SMALL_OWNERS = 12
CHUNKS = 3
CHUNK = 1024
HALF = CHUNK // 2


def shard_index(x_lo, y, core):
    return x_lo * 8 + y * 2 + core


def signal(sem, device):
    pl.semaphore_signal(sem, inc=1, device_id=device, device_id_type=MESH)


def remote(src, dst, send, recv, device):
    return pltpu.make_async_remote_copy(
        src_ref=src, dst_ref=dst, send_sem=send, recv_sem=recv, device_id=device, device_id_type=MESH
    )


def exchange_kernel(
    frames, slot_dest, w, pool, full, outgoing, own_sems, a2a_send, a2a_recv, w_send, w_recv
):
    p, g = lax.axis_index("dp"), lax.axis_index("shard")
    x_lo, y, core = g // 8, (g // 2) % 4, g % 2
    up, down, across = (y + 1) % 4, (y + 3) % 4, (y + 2) % 4
    g_x = shard_index(1 - x_lo, y, core)
    g_up = shard_index(x_lo, up, core)
    g_down = shard_index(x_lo, down, core)
    g_core = shard_index(x_lo, y, 1 - core)

    barrier = pltpu.get_barrier_semaphore()

    def greet(i, carry):
        signal(barrier, ((p + i) % N_DP, g))
        return carry

    lax.fori_loop(1, N_DP, greet, 0)
    for peer in (g_x, g_up, g_down, g_core):
        signal(barrier, (p, peer))

    own_w = pltpu.make_async_copy(w, full.at[g], own_sems.at[0])
    own_w.start()
    pl.semaphore_wait(barrier, N_DP - 1 + 4)

    def send(block, peer, slot, src=None):
        return remote(
            full.at[block] if src is None else src, full.at[block], w_send.at[slot], w_recv.at[slot], (p, peer)
        )

    sent = []

    def go(copy):
        copy.start()
        sent.append(copy)

    go(send(g, g_x, 0, w))
    go(send(g, g_up, 1, w))
    go(send(g, g_down, 2, w))
    go(send(g, g_core, 7, w))

    def source_of(d):
        index = jnp.int32(0)
        for j in range(N_DP):
            index = index + jnp.where(slot_dest[j] == d, j, 0)
        return jnp.minimum(index, N_DP - 1)

    def post(i, carry):
        d = (p + i) % N_DP
        outgoing[i] = frames[source_of(d)]
        remote(outgoing.at[i], pool.at[p], a2a_send.at[i - 1], a2a_recv.at[i - 1], (d, g)).start()
        return carry

    lax.fori_loop(1, N_DP, post, 0)
    outgoing[0] = frames[source_of(p)]
    own_frames = pltpu.make_async_copy(outgoing.at[0], pool.at[p], own_sems.at[1])
    own_frames.start()

    def arrived(block, slot):
        remote(full.at[block], full.at[block], w_send.at[slot], w_recv.at[slot], (p, g_x)).wait_recv()

    arrived(g_x, 0)
    go(send(g_x, g_up, 3))
    go(send(g_x, g_down, 4))
    go(send(g_x, g_core, 8))
    b = shard_index(x_lo, down, core)
    arrived(b, 1)
    go(send(b, g_up, 5))
    go(send(b, g_core, 9))
    b = shard_index(x_lo, up, core)
    arrived(b, 2)
    go(send(b, g_core, 10))
    b = shard_index(1 - x_lo, up, core)
    arrived(b, 4)
    go(send(b, g_down, 6))
    go(send(b, g_core, 11))
    b = shard_index(1 - x_lo, down, core)
    arrived(b, 3)
    go(send(b, g_core, 12))
    b = shard_index(x_lo, across, core)
    arrived(b, 5)
    go(send(b, g_core, 13))
    b = shard_index(1 - x_lo, across, core)
    arrived(b, 6)
    go(send(b, g_core, 14))
    other = 1 - core
    theirs = [
        (x_lo, y, 7), (1 - x_lo, y, 8), (x_lo, down, 9), (x_lo, up, 10),
        (1 - x_lo, up, 11), (1 - x_lo, down, 12), (x_lo, across, 13), (1 - x_lo, across, 14),
    ]
    for bx, by, slot in theirs:
        arrived(shard_index(bx, by, other), slot)

    def collect(i, carry):
        s = (p + N_DP - i) % N_DP
        copy = remote(outgoing.at[i], pool.at[s], a2a_send.at[i - 1], a2a_recv.at[i - 1], (s, g))
        copy.wait_recv()
        copy.wait_send()
        return carry

    lax.fori_loop(1, N_DP, collect, 0)
    for copy in sent:
        copy.wait_send()
    own_frames.wait()
    own_w.wait()


def exchange(frames, slot_dest, w):
    slots, slot_len, width = frames.shape
    rows, cols = w.shape
    return pl.pallas_call(
        exchange_kernel,
        out_shape=(
            jax.ShapeDtypeStruct((slots, slot_len, width), BF),
            jax.ShapeDtypeStruct((N_SHARD, rows, cols), BF),
        ),
        in_specs=[
            pl.BlockSpec(memory_space=pltpu.VMEM),
            pl.BlockSpec(memory_space=pltpu.SMEM),
            pl.BlockSpec(memory_space=pl.ANY),
        ],
        out_specs=(pl.BlockSpec(memory_space=pl.ANY), pl.BlockSpec(memory_space=pl.ANY)),
        scratch_shapes=[
            pltpu.VMEM((slots, slot_len, width), BF),
            pltpu.SemaphoreType.DMA((2,)),
            pltpu.SemaphoreType.DMA((N_DP - 1,)),
            pltpu.SemaphoreType.DMA((N_DP - 1,)),
            pltpu.SemaphoreType.DMA((15,)),
            pltpu.SemaphoreType.DMA((15,)),
        ],
        compiler_params=pltpu.CompilerParams(
            collective_id=0, has_side_effects=True, vmem_limit_bytes=32 * 1024 * 1024
        ),
        name="exchange",
    )(frames, slot_dest, w)


def add_blocks(dst, src, count, cols):
    def step(i, carry):
        block, row = i // 2, pl.multiple_of((i % 2) * 48, 48)
        d, s = dst(block), src(block)
        value = d[pl.ds(row, 48), cols].astype(F32) + s[pl.ds(row, 48), :].astype(F32)
        d[pl.ds(row, 48), cols] = value.astype(BF)
        return carry

    lax.fori_loop(0, count * 2, step, 0)


def reduce_kernel(
    part, small, out, small_out,
    own, rx0, rx1, rx2, rx3, rx4, red, fin, rxs, rxd, small_fin,
    load_sems, s0, r0, s1, r1, s2, r2, s3, r3, s4, r4, s5, r5, st1, rt1, st2, rt2, st3, rt3,
):
    p, g = lax.axis_index("dp"), lax.axis_index("shard")
    z, x_hi = p // 2, p % 2
    x_lo, y, core = g // 8, (g // 2) % 4, g % 2
    y_a, y_b = y + 1 - 2 * (y % 2), 3 - y
    mates = (y_a, y_b)
    scale = 1.0 / (N_DP * N_SHARD)

    def load(k):
        return pltpu.make_async_copy(
            part.at[:, :, core, :, pl.ds(CHUNK * k, CHUNK)], own.at[k], load_sems.at[k]
        )

    for k in range(CHUNKS):
        load(k).start()

    barrier = pltpu.get_barrier_semaphore()

    def greet(i, carry):
        signal(barrier, ((p + i) % N_DP, g))
        signal(barrier, (p, (g + i) % N_SHARD))
        return carry

    lax.fori_loop(1, 16, greet, 0)
    pl.semaphore_wait(barrier, 30)

    def copy0(k):
        return remote(
            part.at[:, :, 1 - core, :, pl.ds(CHUNK * k, CHUNK)], rx0.at[k], s0.at[k], r0.at[k],
            (p, shard_index(x_lo, y, 1 - core)),
        )

    for k in range(CHUNKS):
        copy0(k).start()

    def piece(j):
        return pl.ds(pl.multiple_of(j * 128, 128), 128)

    def send_piece(j, carry):
        @pl.when(j != g)
        def _():
            remote(small.at[:, piece(j)], rxs.at[g], st1.at[j], rt1.at[g], (p, j)).start()

        return carry

    lax.fori_loop(0, SMALL_OWNERS, send_piece, 0)

    def cols(h):
        return pl.ds(HALF * h, HALF)

    def copy1(k, h, j):
        q = mates[h]
        after = 3 - q if h == 0 else q + 1 - 2 * (q % 2)
        block = q if j == 0 else after
        return remote(
            own.at[k, :, block, :, cols(h)], rx1.at[k, h, j], s1.at[k, h, j], r1.at[k, h, j],
            (p, shard_index(x_lo, q, core)),
        )

    for k in range(CHUNKS):
        load(k).wait()
        copy0(k).wait_recv()
        add_blocks(
            lambda i: own.at[k, i // 4, i % 4], lambda i: rx0.at[k, i // 4, i % 4], 8, slice(None)
        )
        for h in range(2):
            for j in (1, 0):
                copy1(k, h, j).start()

    def send_sum(i, carry):
        remote(rxd.at[p], rxd.at[p], st2.at[i - 1], rt2.at[p], ((p + i) % N_DP, g)).start()
        return carry

    @pl.when(g < SMALL_OWNERS)
    def _():
        def take(i, carry):
            s = (g + i) % N_SHARD
            remote(small.at[:, piece(0)], rxs.at[s], st1.at[0], rt1.at[s], (p, s)).wait_recv()
            return carry

        lax.fori_loop(1, N_SHARD, take, 0)
        rxs[g] = small[:, piece(g)]
        total = rxs[0]
        for s in range(1, N_SHARD):
            total = total + rxs[s]
        rxd[p] = total
        lax.fori_loop(1, N_DP, send_sum, 0)

    def copy2(k, h):
        q = mates[1 - h]
        return remote(
            own.at[k, :, q, :, cols(h)], rx2.at[k, h], s2.at[k, h], r2.at[k, h],
            (p, shard_index(x_lo, q, core)),
        )

    for k in range(CHUNKS):
        for h in range(2):
            copy1(k, h, 1).wait_recv()
            add_blocks(lambda i: own.at[k, i, mates[1 - h]], lambda i: rx1.at[k, h, 1, i], 2, cols(h))
            copy2(k, h).start()
            copy1(k, h, 0).wait_recv()
            add_blocks(lambda i: own.at[k, i, y], lambda i: rx1.at[k, h, 0, i], 2, cols(h))

    def send_final(i, carry):
        remote(
            small_fin.at[:, piece(g)], small_fin.at[:, piece(g)], st3.at[i - 1], rt3.at[g],
            (p, (g + i) % N_SHARD),
        ).start()
        return carry

    @pl.when(g < SMALL_OWNERS)
    def _():
        def take(i, carry):
            s = (p + i) % N_DP
            remote(rxd.at[s], rxd.at[s], st2.at[0], rt2.at[s], (s, g)).wait_recv()
            return carry

        lax.fori_loop(1, N_DP, take, 0)
        total = rxd[0]
        for s in range(1, N_DP):
            total = total + rxd[s]
        small_fin[:, piece(g)] = total
        lax.fori_loop(1, N_SHARD, send_final, 0)

    def copy3(k):
        return remote(
            own.at[k, 1 - x_lo, y], rx3.at[k], s3.at[k], r3.at[k], (p, shard_index(1 - x_lo, y, core))
        )

    for k in range(CHUNKS):
        for h in range(2):
            copy2(k, h).wait_recv()
            add_blocks(lambda i: own.at[k, i, y], lambda i: rx2.at[k, h, i], 2, cols(h))
        copy3(k).start()

    def at_piece(ref, d, base):
        return ref.at[
            pl.ds(pl.multiple_of((d % 2) * 48, 48), 48), pl.ds(pl.multiple_of(base + (d // 2) * 128, 128), 128)
        ]

    def copy4(k, i):
        d = (p + i) % N_DP
        return remote(
            at_piece(own.at[k, x_lo, y], d, 0), rx4.at[k, i - 1], s4.at[k, i - 1], r4.at[k, i - 1], (d, g)
        )

    def copy5(k, i):
        d = (p + i) % N_DP
        return remote(
            red.at[k], at_piece(fin, p, CHUNK * k), s5.at[k, i - 1], r5.at[k, i - 1], (d, g)
        )

    for k in range(CHUNKS):
        copy3(k).wait_recv()
        add_blocks(lambda i: own.at[k, x_lo, y], lambda i: rx3.at[k], 1, slice(None))

        def post(i, carry):
            copy4(k, i).start()
            return carry

        lax.fori_loop(1, N_DP, post, 0)

    for k in range(CHUNKS):
        def take(i, carry):
            copy4(k, i).wait_recv()
            return carry

        lax.fori_loop(1, N_DP, take, 0)
        total = at_piece(own.at[k, x_lo, y], p, 0)[...].astype(F32)
        for i in range(N_DP - 1):
            total = total + rx4[k, i].astype(F32)
        total = total.astype(BF)
        red[k] = total
        at_piece(fin, p, CHUNK * k)[...] = total

        def post(i, carry):
            copy5(k, i).start()
            return carry

        lax.fori_loop(1, N_DP, post, 0)

    def take_final(j, carry):
        @pl.when(j != g)
        def _():
            remote(
                small_fin.at[:, piece(j)], small_fin.at[:, piece(j)], st3.at[0], rt3.at[j], (p, j)
            ).wait_recv()

        return carry

    lax.fori_loop(0, SMALL_OWNERS, take_final, 0)
    small_out[...] = small_fin[...] * scale

    for k in range(CHUNKS):
        def take(i, carry):
            s = (p + N_DP - i) % N_DP
            remote(
                red.at[k], at_piece(fin, s, CHUNK * k), s5.at[k, i - 1], r5.at[k, i - 1], (s, g)
            ).wait_recv()
            return carry

        lax.fori_loop(1, N_DP, take, 0)

        def widen(i, carry):
            rows = pl.ds(pl.multiple_of(i * 48, 48), 48)
            out[rows, pl.ds(CHUNK * k, CHUNK)] = fin[rows, pl.ds(CHUNK * k, CHUNK)].astype(F32) * scale
            return carry

        lax.fori_loop(0, 2, widen, 0)

    for k in range(CHUNKS):
        copy0(k).wait_send()
        copy3(k).wait_send()
        for h in range(2):
            copy1(k, h, 0).wait_send()
            copy1(k, h, 1).wait_send()
            copy2(k, h).wait_send()

        def sent(i, carry):
            copy4(k, i).wait_send()
            copy5(k, i).wait_send()
            return carry

        lax.fori_loop(1, N_DP, sent, 0)

    def piece_sent(j, carry):
        @pl.when(j != g)
        def _():
            remote(small.at[:, piece(j)], rxs.at[g], st1.at[j], rt1.at[g], (p, j)).wait_send()

        return carry

    lax.fori_loop(0, SMALL_OWNERS, piece_sent, 0)

    @pl.when(g < SMALL_OWNERS)
    def _():
        def sums_sent(i, carry):
            remote(rxd.at[p], rxd.at[p], st2.at[i - 1], rt2.at[p], (p, g)).wait_send()
            remote(
                small_fin.at[:, piece(g)], small_fin.at[:, piece(g)], st3.at[i - 1], rt3.at[g], (p, g)
            ).wait_send()
            return carry

        lax.fori_loop(1, 16, sums_sent, 0)


def reduce_gradients(part, small):
    rows, cols = part.shape
    block = rows // N_SHARD
    width = small.shape[1]
    dma = pltpu.SemaphoreType.DMA
    return pl.pallas_call(
        reduce_kernel,
        out_shape=(
            jax.ShapeDtypeStruct((block, cols), F32),
            jax.ShapeDtypeStruct((SMALL_ROWS, width), F32),
        ),
        in_specs=[pl.BlockSpec(memory_space=pl.ANY), pl.BlockSpec(memory_space=pltpu.VMEM)],
        out_specs=(pl.BlockSpec(memory_space=pltpu.VMEM), pl.BlockSpec(memory_space=pltpu.VMEM)),
        scratch_shapes=[
            pltpu.VMEM((CHUNKS, 2, 4, block, CHUNK), BF),
            pltpu.VMEM((CHUNKS, 2, 4, block, CHUNK), BF),
            pltpu.VMEM((CHUNKS, 2, 2, 2, block, HALF), BF),
            pltpu.VMEM((CHUNKS, 2, 2, block, HALF), BF),
            pltpu.VMEM((CHUNKS, block, CHUNK), BF),
            pltpu.VMEM((CHUNKS, N_DP - 1, block // 2, 128), BF),
            pltpu.VMEM((CHUNKS, block // 2, 128), BF),
            pltpu.VMEM((block, cols), BF),
            pltpu.VMEM((N_SHARD, SMALL_ROWS, 128), F32),
            pltpu.VMEM((N_DP, SMALL_ROWS, 128), F32),
            pltpu.VMEM((SMALL_ROWS, width), F32),
            dma((CHUNKS,)),
            dma((CHUNKS,)), dma((CHUNKS,)),
            dma((CHUNKS, 2, 2)), dma((CHUNKS, 2, 2)),
            dma((CHUNKS, 2)), dma((CHUNKS, 2)),
            dma((CHUNKS,)), dma((CHUNKS,)),
            dma((CHUNKS, N_DP - 1)), dma((CHUNKS, N_DP - 1)),
            dma((CHUNKS, N_DP - 1)), dma((CHUNKS, N_DP - 1)),
            dma((SMALL_OWNERS,)), dma((N_SHARD,)),
            dma((N_DP - 1,)), dma((N_DP,)),
            dma((N_SHARD - 1,)), dma((SMALL_OWNERS,)),
        ],
        compiler_params=pltpu.CompilerParams(
            collective_id=1, has_side_effects=True, vmem_limit_bytes=40 * 1024 * 1024
        ),
        name="reduce_gradients",
    )(part.reshape(2, 4, 2, block, cols), small)


def gather_frames(pool, lengths, offsets, frame_count, slot_len):
    rows_here = jnp.arange(frame_count, dtype=jnp.int32)[:, None]
    member = ((rows_here >= offsets[None, :]) & (rows_here < (offsets + lengths)[None, :])).astype(
        jnp.int32
    )
    sources = jnp.arange(lengths.shape[0], dtype=jnp.int32)[None, :]
    owner = jnp.sum(member * sources, axis=1)
    within = jnp.sum(member * (rows_here - offsets[None, :]), axis=1)
    picked = jnp.take(pool, owner * slot_len + within, axis=0, mode="clip")
    return (picked, owner)


def normalize(values):
    center = values - jnp.mean(values, axis=1, keepdims=True)
    inverse = lax.rsqrt(jnp.mean(center * center, axis=1, keepdims=True) + EPSILON)
    return (center * inverse, inverse)


def normalize_back(grad_unit, unit, inverse):
    first = jnp.mean(grad_unit, axis=1, keepdims=True)
    second = jnp.mean(grad_unit * unit, axis=1, keepdims=True)
    return inverse * (grad_unit - first - unit * second)


def depth_forward(values, segment, kernel):
    count = values.shape[0]
    reach = (kernel.shape[0] - 1) // 2
    padded = jnp.pad(values, ((reach, reach), (0, 0)))
    labels = jnp.pad(segment, (reach, reach), constant_values=-1)
    total = jnp.zeros_like(values)
    for tap_index in range(kernel.shape[0]):
        same = (labels[tap_index : tap_index + count] == segment)[:, None]
        total = (
            total + jnp.where(same, padded[tap_index : tap_index + count], 0.0) * kernel[tap_index]
        )
    return total


def depth_backward(grads, segment, kernel):
    count = grads.shape[0]
    reach = (kernel.shape[0] - 1) // 2
    padded = jnp.pad(grads, ((reach, reach), (0, 0)))
    labels = jnp.pad(segment, (reach, reach), constant_values=-1)
    total = jnp.zeros_like(grads)
    for tap_index in range(kernel.shape[0]):
        begin = 2 * reach - tap_index
        same = (labels[begin : begin + count] == segment)[:, None]
        total = total + jnp.where(same, padded[begin : begin + count], 0.0) * kernel[tap_index]
    return total


def depth_weight_grad(grads, values, segment, taps_count):
    count = values.shape[0]
    reach = (taps_count - 1) // 2
    padded = jnp.pad(values, ((reach, reach), (0, 0)))
    labels = jnp.pad(segment, (reach, reach), constant_values=-1)
    collected = []
    for tap_index in range(taps_count):
        same = (labels[tap_index : tap_index + count] == segment)[:, None]
        collected.append(
            jnp.sum(jnp.where(same, padded[tap_index : tap_index + count], 0.0) * grads, axis=0)
        )
    return jnp.stack(collected, axis=0)


def body(frames, slot_dest, recv_length, recv_offset, gain1, w_in, w_depth, gain2, cotangent):
    frame_count = cotangent.shape[0]
    slot_len = frames.shape[1]
    model_width = frames.shape[2]
    taps = w_depth.shape[0]
    pool, full = exchange(frames, slot_dest, w_in)
    full_weight = full.reshape(model_width, 2 * model_width)
    inputs, segment = gather_frames(
        pool.reshape(-1, model_width), recv_length, recv_offset, frame_count, slot_len
    )
    unit_in, inverse_in = normalize(inputs.astype(F32))
    normed = (unit_in * gain1).astype(BF)
    projected = jnp.dot(normed, full_weight, preferred_element_type=F32)
    linear = projected[:, :model_width]
    gating = projected[:, model_width:]
    gate_sig = jax.nn.sigmoid(gating)
    gated = (linear * gate_sig).astype(BF)
    gated_wide = gated.astype(F32)
    convolved = depth_forward(gated_wide, segment, w_depth)
    unit_out, inverse_out = normalize(convolved)
    scaled = unit_out * gain2
    sig_out = jax.nn.sigmoid(scaled)
    output = (scaled * sig_out).astype(BF)
    grad_scaled = cotangent.astype(F32) * sig_out * (1.0 + scaled * (1.0 - sig_out))
    gain2_part = jnp.sum(grad_scaled * unit_out, axis=0)
    grad_conv = normalize_back(grad_scaled * gain2, unit_out, inverse_out)
    depth_part = depth_weight_grad(grad_conv, gated_wide, segment, taps)
    grad_gated = depth_backward(grad_conv, segment, w_depth)
    grad_pre = jnp.concatenate(
        [grad_gated * gate_sig, grad_gated * linear * gate_sig * (1.0 - gate_sig)], axis=1
    ).astype(BF)
    grad_normed = lax.dot_general(
        grad_pre, full_weight, (((1,), (1,)), ((), ())), preferred_element_type=F32
    )
    gain1_part = jnp.sum(grad_normed * unit_in, axis=0)
    grad_input = normalize_back(grad_normed * gain1, unit_in, inverse_in).astype(BF)
    weight_part = lax.dot_general(
        normed, grad_pre, (((0,), (0,)), ((), ())), preferred_element_type=F32
    ).astype(BF)
    small = jnp.concatenate(
        [depth_part, gain1_part[None], gain2_part[None], jnp.zeros((SMALL_ROWS - taps - 2, model_width), F32)], axis=0
    )
    grad_w, small_sum = reduce_gradients(weight_part, small)
    return (output, grad_input, grad_w, small_sum[:taps], small_sum[taps], small_sum[taps + 1])


def solution(mesh):
    in_specs = (
        P(("dp", "shard"), None, None),
        P(("dp", "shard")),
        P(("dp", "shard")),
        P(("dp", "shard")),
        P(),
        P("shard", None),
        P(),
        P(),
        P(("dp", "shard"), None),
    )
    out_specs = (
        P(("dp", "shard"), None),
        P(("dp", "shard"), None),
        P("shard", None),
        P(),
        P(),
        P(),
    )
    return jax.shard_map(body, mesh=mesh, in_specs=in_specs, out_specs=out_specs, check_vma=False)
```

time: 747 us -> 246 us (0.33)
  waiting for transfers between devices: 461 us -> 0 us
  Pallas kernels: 0 us -> 149 us
  blocking collectives: 126 us -> 0 us
  other arithmetic: 76.2 us -> 60.1 us
  between operations: 15.3 us -> 1.17 us
  local copies, waits for them, and re-layouts: 27.9 us -> 14.3 us
  starting transfers between devices: 11.7 us -> 0 us
  matrix products: 26.7 us -> 19.2 us
    psum x2 -> x0, waiting for transfers between devices: 400 us -> none  [the longest x1 239 us: body(): lax.psum((gain1_part, gain2_part, depth_part), ('dp', 'shard'))]
    pallas_call x0 -> x2, Pallas kernels: none -> 149 us  [the longest x1 86.3 us: reduce_gradients(): pl.pallas_call(reduce_kernel, out_shape=(jax.ShapeDtypeStruct((block, col...]
    psum x1 -> x0, blocking collectives: 126 us -> none  [body(): lax.psum((gain1_part, gain2_part, depth_part), ('dp', 'shard'))]
    all_to_all x1 -> x0, waiting for transfers between devices: 41.9 us -> none  [body(): lax.all_to_all(outgoing, 'dp', split_axis=0, concat_axis=0, tiled=True)]
    another operation x32 -> x31, local copies, waits for them, and re-layouts: 19.8 us -> 0.2 us  [depth_weight_grad(): return jnp.stack(collected, axis=0)]
    all_gather x1 -> x0, waiting for transfers between devices: 17.8 us -> none  [body(): full_weight = lax.all_gather(w_in, 'shard', axis=0, tiled=True)]
    all_to_all x1 -> x0, starting transfers between devices: 11.6 us -> none  [body(): lax.all_to_all(outgoing, 'dp', split_axis=0, concat_axis=0, tiled=True)]
  transfers between devices with their start and end apart: 5 -> 0, of which waited for: 4 -> 0; matrix products, arithmetic and copies ran while one was open for 9% -> 0% of each run, Pallas kernels for 0% -> 0%
where the time goes in v1:
time: 246 us; the launch traced here: 244 us
  Pallas kernels  149 us (61%)
  other arithmetic  60.1 us (24%)
  matrix products  19.2 us (8%)
  local copies, waits for them, and re-layouts  14.3 us (6%)
    pallas_call x1, Pallas kernels, reduce_gradients(): pl.pallas_call(reduce_kernel, out_shape=(jax.ShapeDtypeStruct((block, col...  86.3 us
    pallas_call x1, Pallas kernels, exchange(): pl.pallas_call(exchange_kernel, out_shape=(jax.ShapeDtypeStruct((slots, s...  63.2 us
    reduce_sum x4, other arithmetic, depth_weight_grad(): jnp.sum(jnp.where(same, padded[tap_index:tap_index + count], 0.0) * grads...  18.5 us
    reduce_sum x2, other arithmetic, normalize(): center = values - jnp.mean(values, axis=1, keepdims=True)  17.4 us
    another operation x2, other arithmetic  16.4 us
    unnamed x31, local copies, waits for them, and re-layouts  9.69 us
    dot_general x1, matrix products, body(): lax.dot_general(normed, grad_pre, (((0,), (0,)), ((), ())), preferred_ele...  7.11 us
    dot_general x1, matrix products, body(): projected = jnp.dot(normed, full_weight, preferred_element_type=F32)  6.48 us

profile of v1, /device:TPU:6, one launch (start us, length us, event | category | flops | bytes accessed | tf_op | source)
XLA Modules:
  0.0 244.2 jit_solution(16139757814446739194)
XLA Ops:
  0.6 0.7 add.227
  1.3 0.7 select_reduce_fusion.1
  2.1 1.5 copy-done
  3.6 1.1 copy-done.1
  4.7 0.7 copy-done.2
  5.3 63.2 %exchange.1 = (bf16[16,40,1536]{2,1,0:T(8,128)(2,1)S(1)}, bf16[16,96,3072]{2,1,0:T(8,128)(2,1)S(1)}) custom-call(bf16[16,40,1536]{2,1,0:T(8,128)(2,1)S(1)} %copy-done, s32[16]{0:T(128)S(1)} %copy-done.2, bf16[96,3072]{1,0:T(8,128)(2,1)S(1)} %copy-done.1), custom_call_target="tpu_custom_call" | custom-call | tf_op jit(solution)/shard_map/exchange/pallas_call | solution.py:146
  68.5 3.6 %copy-done.3 = bf16[16,96,3072]{2,1,0:T(8,128)(2,1)} copy-done((bf16[16,96,3072]{2,1,0:T(8,128)(2,1)}, bf16[16,96,3072]{2,1,0:T(8,128)(2,1)S(1)}, u32[]{:S(2)}) %copy-start.3) | copy-done | bytes 9437208
  72.1 2.2 gather_fusion
  74.6 0.5 fusion.12
  75.1 6.5 %fusion.63 = f32[384,3072]{1,0:T(8,128)S(1)} fusion(bf16[1536,3072]{1,0:T(8,128)(2,1)} %bitcast.7, bf16[384,1536]{1,0:T(8,128)(2,1)S(1)} %gather_fusion, f32[1536]{0:T(1024)S(1)} %copy-done.11, f32[384]{0:T(512)S(1)} %add_rsqrt_fusion.1, f32[384]{0:T(512)S(1)} %broadcast_multiply_fusion.5), kind=kOutput, calls=%fused_computation.235 | convolution fusion | flops 3626827776 | bytes 15344640 | tf_op jit(solution)/shard_map/dot_general | solution.py:554
  81.6 0.6 fusion.58
  82.2 0.3 copy-done.9
  82.5 0.3 slice_reduce_fusion.32
  83.4 17.2 %fusion.65 = (f32[384]{0:T(512)S(1)}, f32[384,1536]{1,0:T(8,128)S(1)}) fusion(f32[1536]{0:T(1024)S(1)} %get-tuple-element.82, pred[384]{0:T(512)(128)(4,1)S(1)} %get-tuple-element.122, f32[1536]{0:T(1024)S(1)} %get-tuple-element.83, pred[384]{0:T(512)(128)(4,1)S(1)} %get-tuple-element.94, f32[1536]{0:T(1024)S(1)} %get-tuple-element.54, ...), kind=kLoop, calls=%fused_computation.236 | loop fusion | flops 54263424 | bytes 4922112 | tf_op jit(solution)/shard_map/reduce_sum | solution.py:490
  100.6 0.4 multiply_reduce_fusion.33
  101.0 0.9 copy-done.7
  101.9 2.7 %multiply_reduce_fusion = (f32[1536]{0:T(1024)S(1)}, f32[384]{0:T(512)S(1)}, f32[384]{0:T(512)S(1)}, f32[384,1536]{1,0:T(8,128)S(1)}, bf16[384,1536]{1,0:T(8,128)(2,1)}) fusion(f32[384,1536]{1,0:T(8,128)S(1)} %get-tuple-element.91, f32[384]{0:T(512)S(1)} %add_rsqrt_fusion, f32[384]{0:T(512)S(1)} %broadcast_multiply_fusion.4, f32[1536]{0:T(1024)S(1)} %copy-done.10, ...), kind=kLoop, calls=%fused_computation.22 | loop fusion | flops 11794176 | bytes 7096320 | tf_op jit(solution)/shard_map/reduce_sum | solution.py:566
  104.6 6.1 %multiply_reduce_fusion.1 = (f32[1536]{0:T(1024)S(1)}, f32[1536]{0:T(1024)S(1)}, f32[1536]{0:T(1024)S(1)}, f32[1536]{0:T(1024)S(1)}, f32[1536]{0:T(1024)S(1)}, /...) fusion(f32[384,1536]{1,0:T(8,128)S(1)} %fusion.58, ...), kind=kLoop, calls=%fused_computation.23 | loop fusion | flops 20040192 | bytes 9508224 | tf_op jit(solution)/shard_map/reduce_sum | solution.py:537
  110.7 5.0 %multiply_reduce_fusion.10 = (f32[1536]{0:T(1024)S(1)}, f32[1536]{0:T(1024)S(1)}, f32[1536]{0:T(1024)S(1)}, f32[1536]{0:T(1024)S(1)}, f32[1536]{0:T(1024)S(1)}, ...) fusion(f32[384,1536]{1,0:T(8,128)S(1)} %get-tuple-element.86, ...), kind=kLoop, calls=%fused_computation.32 | loop fusion | flops 15321600 | bytes 4776960 | tf_op jit(solution)/shard_map/reduce_sum | solution.py:537
  115.9 5.3 %multiply_reduce_fusion.19 = (f32[1536]{0:T(1024)S(1)}, f32[1536]{0:T(1024)S(1)}, f32[1536]{0:T(1024)S(1)}, f32[1536]{0:T(1024)S(1)}, f32[1536]{0:T(1024)S(1)}, ...) fusion(f32[384,1536]{1,0:T(8,128)S(1)} %get-tuple-element.86, ...), kind=kLoop, calls=%fused_computation.41 | loop fusion | flops 15911424 | bytes 4777344 | tf_op jit(solution)/shard_map/reduce_sum | solution.py:537
  121.3 2.1 multiply_reduce_fusion.28
  123.5 15.4 %multiply_convert_fusion.1 = (bf16[384,1536]{1,0:T(8,128)(2,1)}, f32[384,1536]{1,0:T(8,128)S(1)}) fusion(f32[384,3072]{1,0:T(8,128)S(1)} %fusion.63, f32[1536]{0:T(1024)S(1)} %get-tuple-element.82, pred[384]{0:T(512)(128)(4,1)S(1)} %get-tuple-element.93, f32[1536]{0:T(1024)S(1)} %get-tuple-element.83, pred[384]{0:T(512)(128)(4,1)S(1)} %get-tuple-element.102, ...), kind=kLoop, calls=%fused_computation.55 | loop fusion | flops 56623104 | bytes 8459520 | tf_op jit(solution)/shard_map/convert
  138.9 0.9 multiply_convert_fusion
  140.2 0.4 copy-done.5
  140.5 5.6 %fusion.11 = (f32[1536]{0:T(1024)S(1)}, f32[384]{0:T(512)S(1)}, f32[384]{0:T(512)S(1)}, f32[384,1536]{1,0:T(8,128)}) fusion(bf16[384,1536]{1,0:T(8,128)(2,1)S(1)} %gather_fusion, f32[384]{0:T(512)S(1)} %add_rsqrt_fusion.1, f32[384]{0:T(512)S(1)} %broadcast_multiply_fusion.5, f32[1536]{0:T(1024)S(1)} %copy-done.11, bf16[1536,3072]{1,0:T(8,128)(2,1)S(1)} %bitcast.10, ...), kind=kOutput, calls=%fused_computation.15 | convolution fusion | flops 3633903104 | bytes 15353856 | tf_op jit(solution)/shard_map/dot_general | solution.py:573
  146.3 0.4 concatenate.8.small
  146.6 7.1 %convolution_convert_fusion = bf16[1536,3072]{1,0:T(8,128)(2,1)S(1)} fusion(bf16[384,1536]{1,0:T(8,128)(2,1)} %copy-done.8, bf16[384,1536]{1,0:T(8,128)(2,1)S(1)} %copy-done.6, bf16[384,1536]{1,0:T(8,128)(2,1)S(1)} %gather_fusion, f32[1536]{0:T(1024)S(1)} %copy-done.11, f32[384]{0:T(512)S(1)} %add_rsqrt_fusion.1, f32[384]{0:T(512)S(1)} %broadcast_multiply_fusion.5), kind=kOutput, calls=%fused_computation.1 | convolution fusion | flops 3636264960 | bytes 12985344 | tf_op jit(solution)/shard_map/dot_general | solution.py:578
  153.8 86.3 %reduce_gradients.1 = (f32[96,3072]{1,0:T(8,128)S(1)}, f32[40,1536]{1,0:T(8,128)S(1)}) custom-call(bf16[2,4,2,96,3072]{4,3,2,1,0:T(8,128)(2,1)S(1)} %bitcast.6, f32[40,1536]{1,0:T(8,128)S(1)} %concatenate.8.small), custom_call_target="tpu_custom_call" | custom-call | tf_op jit(solution)/shard_map/reduce_gradients/pallas_call | solution.py:439
  240.1 0.7 slice.628
  240.8 0.6 slice_reduce_fusion
  241.4 1.8 fusion.10
  243.1 1.0 copy.16
  (73 shorter events, 1.3 us)
Async XLA Ops:
  2.1 1.5 copy-start
  3.6 1.1 copy-start.1
  4.7 0.7 copy-start.2
  68.5 3.6 %copy-start.3 = (bf16[16,96,3072]{2,1,0:T(8,128)(2,1)}, bf16[16,96,3072]{2,1,0:T(8,128)(2,1)S(1)}, u32[]{:S(2)}) copy-start(bf16[16,96,3072]{2,1,0:T(8,128)(2,1)S(1)} %get-tuple-element.11) | copy-start | bytes 28311556
  74.4 0.7 copy-start.11
  81.6 0.9 copy-start.9
  100.6 1.3 copy-start.7
  100.6 1.3 copy-start.10
  121.3 18.6 %slice-start = ((s8[9437184]{0:T(1024)(128)(4,1)}), s8[4194304]{0:T(1024)(128)(4,1)S(1)}, s32[]{:S(2)}) async-start(s8[9437184]{0:T(1024)(128)(4,1)} %bitcast.8), calls=%async_computation | async-start | bytes 8388608
  123.5 16.4 %slice-start.1 = ((s8[9437184]{0:T(1024)(128)(4,1)}), s8[4194304]{0:T(1024)(128)(4,1)S(1)}, s32[]{:S(2)}) async-start(s8[9437184]{0:T(1024)(128)(4,1)} %bitcast.8), calls=%async_computation.1 | async-start | bytes 8388608
  138.9 1.2 slice-start.2
  138.9 1.6 copy-start.5
  139.9 6.2 %copy-start.8 = (bf16[384,1536]{1,0:T(8,128)(2,1)}, bf16[384,1536]{1,0:T(8,128)(2,1)S(1)}, u32[]{:S(2)}) copy-start(bf16[384,1536]{1,0:T(8,128)(2,1)S(1)} %multiply_convert_fusion) | copy-start | bytes 3538948
  140.5 6.1 %copy-start.6 = (bf16[384,1536]{1,0:T(8,128)(2,1)S(1)}, bf16[384,1536]{1,0:T(8,128)(2,1)}, u32[]{:S(2)}) copy-start(bf16[384,1536]{1,0:T(8,128)(2,1)} %get-tuple-element.87) | copy-start | bytes 3538948
  153.8 87.6 %copy-start.4 = (f32[384,1536]{1,0:T(8,128)S(1)}, f32[384,1536]{1,0:T(8,128)}, u32[]{:S(2)}) copy-start(f32[384,1536]{1,0:T(8,128)} %get-tuple-element.123) | copy-start | bytes 7077892

commit v2 on v1

--- a/solution.py
+++ b/solution.py
@@ -195,7 +195,7 @@
 
     def load(k):
         return pltpu.make_async_copy(
-            part.at[:, :, core, :, pl.ds(CHUNK * k, CHUNK)], own.at[k], load_sems.at[k]
+            part.at[k, :, :, core], own.at[k], load_sems.at[k]
         )
 
     for k in range(CHUNKS):
@@ -213,7 +213,7 @@
 
     def copy0(k):
         return remote(
-            part.at[:, :, 1 - core, :, pl.ds(CHUNK * k, CHUNK)], rx0.at[k], s0.at[k], r0.at[k],
+            part.at[k, :, :, 1 - core], rx0.at[k], s0.at[k], r0.at[k],
             (p, shard_index(x_lo, y, 1 - core)),
         )
 
@@ -390,7 +390,10 @@
 
         def widen(i, carry):
             rows = pl.ds(pl.multiple_of(i * 48, 48), 48)
-            out[rows, pl.ds(CHUNK * k, CHUNK)] = fin[rows, pl.ds(CHUNK * k, CHUNK)].astype(F32) * scale
+            for h in range(2):
+                out[rows, pl.ds(h * WIDTH + HALF * k, HALF)] = (
+                    fin[rows, pl.ds(CHUNK * k + HALF * h, HALF)].astype(F32) * scale
+                )
             return carry
 
         lax.fori_loop(0, 2, widen, 0)
@@ -432,8 +435,7 @@
 
 
 def reduce_gradients(part, small):
-    rows, cols = part.shape
-    block = rows // N_SHARD
+    block, cols = part.shape[4], CHUNKS * part.shape[5]
     width = small.shape[1]
     dma = pltpu.SemaphoreType.DMA
     return pl.pallas_call(
@@ -471,117 +473,336 @@
             collective_id=1, has_side_effects=True, vmem_limit_bytes=40 * 1024 * 1024
         ),
         name="reduce_gradients",
-    )(part.reshape(2, 4, 2, block, cols), small)
-
-
-def gather_frames(pool, lengths, offsets, frame_count, slot_len):
-    rows_here = jnp.arange(frame_count, dtype=jnp.int32)[:, None]
-    member = ((rows_here >= offsets[None, :]) & (rows_here < (offsets + lengths)[None, :])).astype(
-        jnp.int32
-    )
-    sources = jnp.arange(lengths.shape[0], dtype=jnp.int32)[None, :]
-    owner = jnp.sum(member * sources, axis=1)
-    within = jnp.sum(member * (rows_here - offsets[None, :]), axis=1)
-    picked = jnp.take(pool, owner * slot_len + within, axis=0, mode="clip")
-    return (picked, owner)
-
-
-def normalize(values):
-    center = values - jnp.mean(values, axis=1, keepdims=True)
-    inverse = lax.rsqrt(jnp.mean(center * center, axis=1, keepdims=True) + EPSILON)
-    return (center * inverse, inverse)
-
-
-def normalize_back(grad_unit, unit, inverse):
-    first = jnp.mean(grad_unit, axis=1, keepdims=True)
-    second = jnp.mean(grad_unit * unit, axis=1, keepdims=True)
-    return inverse * (grad_unit - first - unit * second)
-
-
-def depth_forward(values, segment, kernel):
-    count = values.shape[0]
-    reach = (kernel.shape[0] - 1) // 2
-    padded = jnp.pad(values, ((reach, reach), (0, 0)))
-    labels = jnp.pad(segment, (reach, reach), constant_values=-1)
-    total = jnp.zeros_like(values)
-    for tap_index in range(kernel.shape[0]):
-        same = (labels[tap_index : tap_index + count] == segment)[:, None]
-        total = (
-            total + jnp.where(same, padded[tap_index : tap_index + count], 0.0) * kernel[tap_index]
-        )
-    return total
-
-
-def depth_backward(grads, segment, kernel):
-    count = grads.shape[0]
-    reach = (kernel.shape[0] - 1) // 2
-    padded = jnp.pad(grads, ((reach, reach), (0, 0)))
-    labels = jnp.pad(segment, (reach, reach), constant_values=-1)
-    total = jnp.zeros_like(grads)
-    for tap_index in range(kernel.shape[0]):
-        begin = 2 * reach - tap_index
-        same = (labels[begin : begin + count] == segment)[:, None]
-        total = total + jnp.where(same, padded[begin : begin + count], 0.0) * kernel[tap_index]
-    return total
-
-
-def depth_weight_grad(grads, values, segment, taps_count):
-    count = values.shape[0]
-    reach = (taps_count - 1) // 2
-    padded = jnp.pad(values, ((reach, reach), (0, 0)))
-    labels = jnp.pad(segment, (reach, reach), constant_values=-1)
-    collected = []
-    for tap_index in range(taps_count):
-        same = (labels[tap_index : tap_index + count] == segment)[:, None]
-        collected.append(
-            jnp.sum(jnp.where(same, padded[tap_index : tap_index + count], 0.0) * grads, axis=0)
-        )
-    return jnp.stack(collected, axis=0)
+    )(part, small)
+
+
+ROWS = 384
+WIDTH = 1536
+TAPS = 31
+REACH = 15
+PAD = 16
+LANES = 128
+BLOCKS = WIDTH // LANES
+TILE = 256
+GROUP = 48
+
+
+def sigmoid(v):
+    return 1.0 / (1.0 + jnp.exp(-v))
+
+
+def dot(a, b):
+    return lax.dot_general(a, b, (((1,), (0,)), ((), ())), preferred_element_type=F32)
+
+
+def dot_t(a, b):
+    return lax.dot_general(a, b, (((1,), (1,)), ((), ())), preferred_element_type=F32)
+
+
+def row_mean(blocks):
+    total = blocks[0]
+    for b in blocks[1:]:
+        total = total + b
+    return jnp.sum(total, axis=1, keepdims=True) * (1.0 / WIDTH)
+
+
+def lanes(b):
+    return pl.ds(b * LANES, LANES)
+
+
+def load_inputs(lengths, offsets, pool, gain1, r):
+    slot_len = pool.shape[0] // N_DP
+    rows = lax.broadcasted_iota(jnp.int32, (ROWS, LANES), 0)
+    pick = jnp.zeros((ROWS, LANES), jnp.int32)
+    behind = jnp.zeros((ROWS, LANES), jnp.int32)
+    ahead = jnp.zeros((ROWS, LANES), jnp.int32)
+    for s in range(N_DP):
+        begin = offsets[s]
+        end = begin + lengths[s]
+        inside = (rows >= begin) & (rows < end)
+        pick = jnp.where(inside, rows - begin + s * slot_len, pick)
+        behind = jnp.where(inside, rows - begin, behind)
+        ahead = jnp.where(inside, end - 1 - rows, ahead)
+    r["behind"][...] = behind
+    r["ahead"][...] = ahead
+    lane = lax.broadcasted_iota(jnp.int32, (ROWS, LANES), 1)
+    for t in range(pool.shape[0] // LANES):
+        r["chosen"][:, lanes(t)] = (pick == lane + t * LANES).astype(F32).astype(BF)
+
+    def gather(t, carry):
+        cols = pl.ds(pl.multiple_of(t * TILE, TILE), TILE)
+        r["unit_in"][:, cols] = dot(r["chosen"][...], pool[:, cols])
+        return carry
+
+    lax.fori_loop(0, WIDTH // TILE, gather, 0)
+
+    def norm(i, carry):
+        rows = pl.ds(pl.multiple_of(i * 16, 16), 16)
+        x = [r["unit_in"][rows, lanes(b)] for b in range(BLOCKS)]
+        mean = row_mean(x)
+        x = [v - mean for v in x]
+        inverse = lax.rsqrt(row_mean([v * v for v in x]) + EPSILON)
+        r["inv_in"][rows, :] = jnp.broadcast_to(inverse, (16, LANES))
+        for b in range(BLOCKS):
+            unit = x[b] * inverse
+            r["unit_in"][rows, lanes(b)] = unit
+            r["normed"][rows, lanes(b)] = (unit * gain1[:, lanes(b)]).astype(BF)
+        return carry
+
+    lax.fori_loop(0, ROWS // 16, norm, 0)
+
+
+def transpose_normed(r):
+    for b in range(BLOCKS):
+        r["normed_t"][lanes(b), :] = r["normed"][:, lanes(b)].T
+
+
+def project(w, wait_tile, r):
+    def tile(t, carry):
+        wait_tile(t)
+        cols = pl.ds(pl.multiple_of(t * TILE, TILE), TILE)
+        gates = pl.ds(pl.multiple_of(t * TILE + WIDTH, TILE), TILE)
+        linear = dot(r["normed"][...], w[:, cols])
+        sig = sigmoid(dot(r["normed"][...], w[:, gates]))
+        r["linear"][:, cols] = linear
+        r["sig"][:, cols] = sig
+        gated = (linear * sig).astype(BF).astype(F32)
+        for j in range(TILE // LANES):
+            r["gated"][t * (TILE // LANES) + j, PAD : PAD + ROWS, :] = gated[:, j * LANES : (j + 1) * LANES]
+        return carry
+
+    lax.fori_loop(0, WIDTH // TILE, tile, 0)
+
+
+def tap_mask(behind, ahead, shift):
+    return ahead >= shift if shift > 0 else behind >= -shift
+
+
+def convolve(w_depth, r):
+    def pair(c, carry):
+        for g in range(ROWS // GROUP):
+            begin = g * GROUP
+            behind = r["behind"][begin : begin + GROUP, :]
+            ahead = r["ahead"][begin : begin + GROUP, :]
+            total = [jnp.zeros((GROUP, LANES), F32)] * 2
+            for k in range(TAPS):
+                shift = k - REACH
+                same = tap_mask(behind, ahead, shift)
+                for j in range(2):
+                    b = c * 2 + j
+                    x = r["gated"][b, PAD + begin + shift : PAD + begin + shift + GROUP, :]
+                    if shift != 0:
+                        x = jnp.where(same, x, 0.0)
+                    total[j] = total[j] + x * w_depth[b, k : k + 1, :]
+            for j in range(2):
+                r["conv"][c * 2 + j, PAD + begin : PAD + begin + GROUP, :] = total[j]
+        return carry
+
+    lax.fori_loop(0, BLOCKS // 2, pair, 0)
+
+
+def finish_forward(gain2, cotangent, output, r):
+    r["gain2_sum"][...] = jnp.zeros_like(r["gain2_sum"])
+
+    def rows16(i, carry):
+        rows = pl.ds(pl.multiple_of(i * 16, 16), 16)
+        held = pl.ds(pl.multiple_of(i * 16 + PAD, 16), 16)
+        x = [r["conv"][b, held, :] for b in range(BLOCKS)]
+        mean = row_mean(x)
+        x = [v - mean for v in x]
+        inverse = lax.rsqrt(row_mean([v * v for v in x]) + EPSILON)
+        units, grads = [], []
+        for b in range(BLOCKS):
+            unit = x[b] * inverse
+            gain = gain2[:, lanes(b)]
+            scaled = unit * gain
+            sig = sigmoid(scaled)
+            output[rows, lanes(b)] = (scaled * sig).astype(BF)
+            grad = cotangent[rows, lanes(b)].astype(F32) * sig * (1.0 + scaled * (1.0 - sig))
+            both = grad * unit
+            r["gain2_sum"][b] = r["gain2_sum"][b] + (both[:8] + both[8:])
+            units.append(unit)
+            grads.append(grad * gain)
+        first = row_mean(grads)
+        second = row_mean([q * u for q, u in zip(grads, units)])
+        for b in range(BLOCKS):
+            r["conv"][b, held, :] = inverse * (grads[b] - first - units[b] * second)
+        return carry
+
+    lax.fori_loop(0, ROWS // 16, rows16, 0)
+
+
+def back_convolve(chunk, w_depth, small, r):
+    def pair(c, carry):
+        first = chunk * (HALF // LANES) + c * 2
+        r["tap_sum"][...] = jnp.zeros_like(r["tap_sum"])
+        for g in range(ROWS // GROUP):
+            begin = g * GROUP
+            rows = slice(begin, begin + GROUP)
+            behind = r["behind"][rows, :]
+            ahead = r["ahead"][rows, :]
+            total = [jnp.zeros((GROUP, LANES), F32)] * 2
+            gated = [r["gated"][first + j, PAD + begin : PAD + begin + GROUP, :] for j in range(2)]
+            for k in range(TAPS):
+                shift = REACH - k
+                same = tap_mask(behind, ahead, shift)
+                for j in range(2):
+                    x = r["conv"][first + j, PAD + begin + shift : PAD + begin + shift + GROUP, :]
+                    if shift != 0:
+                        x = jnp.where(same, x, 0.0)
+                    total[j] = total[j] + x * w_depth[first + j, k : k + 1, :]
+                    product = x * gated[j]
+                    part = product[0:8]
+                    for q in range(1, GROUP // 8):
+                        part = part + product[q * 8 : (q + 1) * 8]
+                    r["tap_sum"][j, k] = r["tap_sum"][j, k] + part
+            for j in range(2):
+                at = pl.multiple_of((first + j) * LANES, LANES)
+                linear = r["linear"][rows, pl.ds(at, LANES)]
+                sig = r["sig"][rows, pl.ds(at, LANES)]
+                grad = total[j] * sig
+                r["grad_pre"][rows, pl.ds(at, LANES)] = grad.astype(BF)
+                r["grad_pre"][rows, pl.ds(at + WIDTH, LANES)] = (grad * linear * (1.0 - sig)).astype(BF)
+        for j in range(2):
+            at = pl.multiple_of((first + j) * LANES, LANES)
+            small[0:TAPS, pl.ds(at, LANES)] = jnp.sum(r["tap_sum"][j], axis=1)
+        return carry
+
+    lax.fori_loop(0, HALF // LANES // 2, pair, 0)
+
+
+def weight_term(chunk, part, r):
+    def tile(i, carry):
+        rows = pl.ds(pl.multiple_of(i * 384, 384), 384)
+        for h in range(2):
+            cols = pl.ds(h * WIDTH + chunk * HALF, HALF)
+            value = dot(r["normed_t"][rows, :], r["grad_pre"][:, cols]).astype(BF)
+            for q in range(4):
+                part[i // 2, (i % 2) * 2 + q // 2, q % 2, :, h * HALF : (h + 1) * HALF] = value[q * 96 : (q + 1) * 96]
+        return carry
+
+    lax.fori_loop(0, 4, tile, 0)
+
+
+def finish_back(w, gain1, grad_input, small, r):
+    def tile(t, carry):
+        cols = pl.ds(pl.multiple_of(t * TILE, TILE), TILE)
+        r["linear"][:, cols] = dot_t(r["grad_pre"][...], w[cols, :])
+        return carry
+
+    lax.fori_loop(0, WIDTH // TILE, tile, 0)
+    r["gain1_sum"][...] = jnp.zeros_like(r["gain1_sum"])
+
+    def rows16(i, carry):
+        rows = pl.ds(pl.multiple_of(i * 16, 16), 16)
+        inverse = r["inv_in"][rows, :]
+        units = [r["unit_in"][rows, lanes(b)] for b in range(BLOCKS)]
+        grads = [r["linear"][rows, lanes(b)] for b in range(BLOCKS)]
+        for b in range(BLOCKS):
+            both = grads[b] * units[b]
+            r["gain1_sum"][b] = r["gain1_sum"][b] + (both[:8] + both[8:])
+        grads = [grads[b] * gain1[:, lanes(b)] for b in range(BLOCKS)]
+        first = row_mean(grads)
+        second = row_mean([q * u for q, u in zip(grads, units)])
+        for b in range(BLOCKS):
+            grad_input[rows, lanes(b)] = (inverse * (grads[b] - first - units[b] * second)).astype(BF)
+        return carry
+
+    lax.fori_loop(0, ROWS // 16, rows16, 0)
+    for b in range(BLOCKS):
+        small[TAPS : TAPS + 1, lanes(b)] = jnp.sum(r["gain1_sum"][b], axis=0, keepdims=True)
+        small[TAPS + 1 : TAPS + 2, lanes(b)] = jnp.sum(r["gain2_sum"][b], axis=0, keepdims=True)
+    small[TAPS + 2 : SMALL_ROWS, :] = jnp.zeros((SMALL_ROWS - TAPS - 2, WIDTH), F32)
+
+
+WORK = (
+    ("behind", (ROWS, LANES), jnp.int32),
+    ("ahead", (ROWS, LANES), jnp.int32),
+    ("chosen", (ROWS, 640), BF),
+    ("unit_in", (ROWS, WIDTH), F32),
+    ("inv_in", (ROWS, LANES), F32),
+    ("normed", (ROWS, WIDTH), BF),
+    ("normed_t", (WIDTH, ROWS), BF),
+    ("linear", (ROWS, WIDTH), F32),
+    ("sig", (ROWS, WIDTH), F32),
+    ("gated", (BLOCKS, PAD + ROWS + PAD, LANES), F32),
+    ("conv", (BLOCKS, PAD + ROWS + PAD, LANES), F32),
+    ("gain1_sum", (BLOCKS, 8, LANES), F32),
+    ("gain2_sum", (BLOCKS, 8, LANES), F32),
+    ("tap_sum", (2, TAPS, 8, LANES), F32),
+    ("grad_pre", (ROWS, 2 * WIDTH), BF),
+)
+
+
+def forward(lengths, offsets, pool, w_hbm, gain1, w_depth, gain2, cotangent, output, w, w_sems, r):
+    def copy_w(t, h):
+        cols = pl.ds(pl.multiple_of(t * TILE + h * WIDTH, TILE), TILE)
+        return pltpu.make_async_copy(w_hbm.at[:, cols], w.at[:, cols], w_sems.at[h, t])
+
+    for t in range(WIDTH // TILE):
+        for h in range(2):
+            copy_w(t, h).start()
+
+    def wait_tile(t):
+        for h in range(2):
+            copy_w(t, h).wait()
+
+    for name in ("gated", "conv"):
+        r[name][:, 0:PAD, :] = jnp.zeros((BLOCKS, PAD, LANES), F32)
+        r[name][:, PAD + ROWS :, :] = jnp.zeros((BLOCKS, PAD, LANES), F32)
+    load_inputs(lengths, offsets, pool, gain1, r)
+    project(w, wait_tile, r)
+    convolve(w_depth, r)
+    finish_forward(gain2, cotangent, output, r)
+    transpose_normed(r)
+
+
+def module_kernel(
+    lengths, offsets, pool, w_hbm, gain1, w_depth, gain2, cotangent,
+    output, grad_input, part, small, w, w_sems, *work
+):
+    r = {name: ref for (name, _, _), ref in zip(WORK, work)}
+    forward(lengths, offsets, pool, w_hbm, gain1, w_depth, gain2, cotangent, output, w, w_sems, r)
+    for chunk in range(CHUNKS):
+        back_convolve(chunk, w_depth, small, r)
+        weight_term(chunk, part.at[chunk], r)
+    finish_back(w, gain1, grad_input, small, r)
+
+
+def module(lengths, offsets, pool, full, gain1, w_depth, gain2, cotangent):
+    vmem = pl.BlockSpec(memory_space=pltpu.VMEM)
+    smem = pl.BlockSpec(memory_space=pltpu.SMEM)
+    block = WIDTH // N_SHARD
+    return pl.pallas_call(
+        module_kernel,
+        out_shape=(
+            jax.ShapeDtypeStruct((ROWS, WIDTH), BF),
+            jax.ShapeDtypeStruct((ROWS, WIDTH), BF),
+            jax.ShapeDtypeStruct((CHUNKS, 2, 4, 2, block, CHUNK), BF),
+            jax.ShapeDtypeStruct((SMALL_ROWS, WIDTH), F32),
+        ),
+        in_specs=[smem, smem, vmem, pl.BlockSpec(memory_space=pl.ANY), vmem, vmem, vmem, vmem],
+        out_specs=(vmem,) * 4,
+        scratch_shapes=[
+            pltpu.VMEM((WIDTH, 2 * WIDTH), BF),
+            pltpu.SemaphoreType.DMA((2, WIDTH // TILE)),
+            *[pltpu.VMEM(shape, dtype) for _, shape, dtype in WORK],
+        ],
+        compiler_params=pltpu.CompilerParams(vmem_limit_bytes=58 * 1024 * 1024),
+        name="module",
+    )(lengths, offsets, pool, full, gain1, w_depth, gain2, cotangent)
 
 
 def body(frames, slot_dest, recv_length, recv_offset, gain1, w_in, w_depth, gain2, cotangent):
-    frame_count = cotangent.shape[0]
-    slot_len = frames.shape[1]
     model_width = frames.shape[2]
     taps = w_depth.shape[0]
     pool, full = exchange(frames, slot_dest, w_in)
-    full_weight = full.reshape(model_width, 2 * model_width)
-    inputs, segment = gather_frames(
-        pool.reshape(-1, model_width), recv_length, recv_offset, frame_count, slot_len
+    blocked = w_depth.reshape(taps, BLOCKS, LANES).transpose(1, 0, 2)
+    output, grad_input, part, small = module(
+        recv_length, recv_offset, pool.reshape(-1, model_width), full.reshape(model_width, 2 * model_width),
+        gain1[None], blocked, gain2[None], cotangent,
     )
-    unit_in, inverse_in = normalize(inputs.astype(F32))
-    normed = (unit_in * gain1).astype(BF)
-    projected = jnp.dot(normed, full_weight, preferred_element_type=F32)
-    linear = projected[:, :model_width]
-    gating = projected[:, model_width:]
-    gate_sig = jax.nn.sigmoid(gating)
-    gated = (linear * gate_sig).astype(BF)
-    gated_wide = gated.astype(F32)
-    convolved = depth_forward(gated_wide, segment, w_depth)
-    unit_out, inverse_out = normalize(convolved)
-    scaled = unit_out * gain2
-    sig_out = jax.nn.sigmoid(scaled)
-    output = (scaled * sig_out).astype(BF)
-    grad_scaled = cotangent.astype(F32) * sig_out * (1.0 + scaled * (1.0 - sig_out))
-    gain2_part = jnp.sum(grad_scaled * unit_out, axis=0)
-    grad_conv = normalize_back(grad_scaled * gain2, unit_out, inverse_out)
-    depth_part = depth_weight_grad(grad_conv, gated_wide, segment, taps)
-    grad_gated = depth_backward(grad_conv, segment, w_depth)
-    grad_pre = jnp.concatenate(
-        [grad_gated * gate_sig, grad_gated * linear * gate_sig * (1.0 - gate_sig)], axis=1
-    ).astype(BF)
-    grad_normed = lax.dot_general(
-        grad_pre, full_weight, (((1,), (1,)), ((), ())), preferred_element_type=F32
-    )
-    gain1_part = jnp.sum(grad_normed * unit_in, axis=0)
-    grad_input = normalize_back(grad_normed * gain1, unit_in, inverse_in).astype(BF)
-    weight_part = lax.dot_general(
-        normed, grad_pre, (((0,), (0,)), ((), ())), preferred_element_type=F32
-    ).astype(BF)
-    small = jnp.concatenate(
-        [depth_part, gain1_part[None], gain2_part[None], jnp.zeros((SMALL_ROWS - taps - 2, model_width), F32)], axis=0
-    )
-    grad_w, small_sum = reduce_gradients(weight_part, small)
+    grad_w, small_sum = reduce_gradients(part, small)
     return (output, grad_input, grad_w, small_sum[:taps], small_sum[taps], small_sum[taps + 1])
 
 

time: 246 us -> 238 us (0.967)
  Pallas kernels: 149 us -> 217 us
  other arithmetic: 60.1 us -> 0 us
  matrix products: 19.2 us -> 0 us
  local copies, waits for them, and re-layouts: 14.3 us -> 18.4 us
    pallas_call x0 -> x1, Pallas kernels: none -> 68.6 us  [module(): pl.pallas_call(module_kernel, out_shape=(jax.ShapeDtypeStruct((ROWS, WIDT...]
    reduce_sum x10 -> x0, other arithmetic: 40.3 us -> none  [the longest x4 18.5 us: depth_weight_grad(): jnp.sum(jnp.where(same, padded[tap_index:tap_index + count], 0.0) * grads...]
    dot_general x3 -> x0, matrix products: 19.2 us -> none  [the longest x1 7.11 us: body(): lax.dot_general(normed, grad_pre, (((0,), (0,)), ((), ())), preferred_ele...]
    another operation x2 -> x0, other arithmetic: 16.4 us -> none
    unnamed x31 -> x15, local copies, waits for them, and re-layouts: 9.69 us -> 12.7 us
    broadcast_in_dim x3 -> x2, local copies, waits for them, and re-layouts: 0.02 us -> 2.65 us  [the longest x1 1.36 us: body(): gain1[None]]
where the time goes in v2:
time: 238 us; the launch traced here: 236 us
  Pallas kernels  217 us (91%)
  local copies, waits for them, and re-layouts  18.4 us (8%)
    pallas_call x1, Pallas kernels, reduce_gradients(): pl.pallas_call(reduce_kernel, out_shape=(jax.ShapeDtypeStruct((block, col...  85.5 us
    pallas_call x1, Pallas kernels, module(): pl.pallas_call(module_kernel, out_shape=(jax.ShapeDtypeStruct((ROWS, WIDT...  68.6 us
    pallas_call x1, Pallas kernels, exchange(): pl.pallas_call(exchange_kernel, out_shape=(jax.ShapeDtypeStruct((slots, s...  63.2 us
    unnamed x15, local copies, waits for them, and re-layouts  12.7 us

profile of v2, /device:TPU:6, one launch (start us, length us, event | category | flops | bytes accessed | tf_op | source)
XLA Modules:
  0.0 236.4 jit_solution(12942418489344089698)
XLA Ops:
  0.6 0.0 copy-start.4
  0.6 1.4 broadcast_in_dim.6.gain1
  2.0 1.3 broadcast_in_dim.7.gain2
  3.3 1.0 reshape.23
  4.3 0.7 copy.17
  5.0 0.0 copy-done.4
  5.0 0.0 copy-start.2
  5.0 1.5 copy-done.2
  6.6 0.0 copy-start.6
  6.6 0.7 copy-done.6
  7.2 63.2 %exchange.1 = (bf16[16,40,1536]{2,1,0:T(8,128)(2,1)S(1)}, bf16[16,96,3072]{2,1,0:T(8,128)(2,1)S(1)}) custom-call(bf16[16,40,1536]{2,1,0:T(8,128)(2,1)S(1)} %copy-done.2, s32[16]{0:T(128)S(1)} %copy-done.6, bf16[96,3072]{1,0:T(8,128)(2,1)S(1)} %copy-done.4), custom_call_target="tpu_custom_call" | custom-call | tf_op jit(solution)/shard_map/exchange/pallas_call | solution.py:146
  70.4 0.0 copy-start.1
  70.4 3.6 %copy-done.1 = bf16[16,96,3072]{2,1,0:T(8,128)(2,1)} copy-done((bf16[16,96,3072]{2,1,0:T(8,128)(2,1)}, bf16[16,96,3072]{2,1,0:T(8,128)(2,1)S(1)}, u32[]{:S(2)}) %copy-start.1) | copy-done | bytes 9437208
  74.0 0.0 copy-start.3
  74.0 1.3 copy-done.3
  75.3 68.6 %module.1 = (bf16[384,1536]{1,0:T(8,128)(2,1)}, bf16[384,1536]{1,0:T(8,128)(2,1)}, bf16[3,2,4,2,96,1024]{5,4,3,2,1,0:T(8,128)(2,1)}, f32[40,1536]{1,0:T(8,128)}) custom-call(s32[16]{0:T(128)} %lengths.1, s32[16]{0:T(128)} %offsets.1, bf16[640,1536]{1,0:T(8,128)(2,1)} %bitcast.6, bf16[1536,3072]{1,0:T(8,128)(2,1)} %bitcast.5, ...), custom_call_target="tpu_custom_call" | custom-call | tf_op jit(solution)/shard_map/module/pallas_call | solution.py:776
  143.8 0.0 copy-start
  143.9 3.7 %copy-done = bf16[3,2,4,2,96,1024]{5,4,3,2,1,0:T(8,128)(2,1)S(1)} copy-done((bf16[3,2,4,2,96,1024]{5,4,3,2,1,0:T(8,128)(2,1)S(1)}, bf16[3,2,4,2,96,1024]{5,4,3,2,1,0:T(8,128)(2,1)}, u32[]{:S(2)}) %copy-start) | copy-done | bytes 9437208
  147.5 0.0 copy-start.5
  147.5 0.9 copy-done.5
  148.5 85.5 %reduce_gradients.1 = (f32[96,3072]{1,0:T(8,128)S(1)}, f32[40,1536]{1,0:T(8,128)S(1)}) custom-call(bf16[3,2,4,2,96,1024]{5,4,3,2,1,0:T(8,128)(2,1)S(1)} %copy-done, f32[40,1536]{1,0:T(8,128)S(1)} %copy-done.5), custom_call_target="tpu_custom_call" | custom-call | tf_op jit(solution)/shard_map/reduce_gradients/pallas_call | solution.py:441
  234.0 0.6 slice_reduce_fusion
  234.7 0.7 slice.9
  235.3 1.0 copy.19
Async XLA Ops:
  0.6 4.4 %copy-start.4 = (bf16[96,3072]{1,0:T(8,128)(2,1)S(1)}, bf16[96,3072]{1,0:T(8,128)(2,1)}, u32[]{:S(2)}) copy-start(bf16[96,3072]{1,0:T(8,128)(2,1)} %w.1) | copy-start | bytes 1769476
  5.0 1.5 copy-start.2
  6.6 0.7 copy-start.6
  70.4 3.6 %copy-start.1 = (bf16[16,96,3072]{2,1,0:T(8,128)(2,1)}, bf16[16,96,3072]{2,1,0:T(8,128)(2,1)S(1)}, u32[]{:S(2)}) copy-start(bf16[16,96,3072]{2,1,0:T(8,128)(2,1)S(1)} %get-tuple-element.15) | copy-start | bytes 28311556
  74.0 1.3 copy-start.3
  143.8 3.7 %copy-start = (bf16[3,2,4,2,96,1024]{5,4,3,2,1,0:T(8,128)(2,1)S(1)}, bf16[3,2,4,2,96,1024]{5,4,3,2,1,0:T(8,128)(2,1)}, u32[]{:S(2)}) copy-start(bf16[3,2,4,2,96,1024]{5,4,3,2,1,0:T(8,128)(2,1)} %get-tuple-element.18.part) | copy-start | bytes 28311556
  147.5 0.9 copy-start.5

commit v3 on v2

v3 whole, which is shorter than its diff:
```python
import jax
import jax.numpy as jnp
from jax import lax
from jax.experimental import pallas as pl
from jax.experimental.pallas import tpu as pltpu
from jax.sharding import PartitionSpec as P

EPSILON = 1e-05
MESH = pl.DeviceIdType.MESH
BF = jnp.bfloat16
F32 = jnp.float32

N_DP = 16
N_SHARD = 16
SMALL_ROWS = 40
SMALL_OWNERS = 12
CHUNKS = 3
CHUNK = 1024
HALF = CHUNK // 2


def shard_index(x_lo, y, core):
    return x_lo * 8 + y * 2 + core


def signal(sem, device):
    pl.semaphore_signal(sem, inc=1, device_id=device, device_id_type=MESH)


def remote(src, dst, send, recv, device):
    return pltpu.make_async_remote_copy(
        src_ref=src, dst_ref=dst, send_sem=send, recv_sem=recv, device_id=device, device_id_type=MESH
    )


def exchange_kernel(
    frames, slot_dest, w, pool, full, outgoing, own_sems, a2a_send, a2a_recv, w_send, w_recv
):
    p, g = lax.axis_index("dp"), lax.axis_index("shard")
    x_lo, y, core = g // 8, (g // 2) % 4, g % 2
    up, down, across = (y + 1) % 4, (y + 3) % 4, (y + 2) % 4
    g_x = shard_index(1 - x_lo, y, core)
    g_up = shard_index(x_lo, up, core)
    g_down = shard_index(x_lo, down, core)
    g_core = shard_index(x_lo, y, 1 - core)

    barrier = pltpu.get_barrier_semaphore()

    def greet(i, carry):
        signal(barrier, ((p + i) % N_DP, g))
        return carry

    lax.fori_loop(1, N_DP, greet, 0)
    for peer in (g_x, g_up, g_down, g_core):
        signal(barrier, (p, peer))

    own_w = pltpu.make_async_copy(w, full.at[g], own_sems.at[0])
    own_w.start()
    pl.semaphore_wait(barrier, N_DP - 1 + 4)

    def send(block, peer, slot, src=None):
        return remote(
            full.at[block] if src is None else src, full.at[block], w_send.at[slot], w_recv.at[slot], (p, peer)
        )

    sent = []

    def go(copy):
        copy.start()
        sent.append(copy)

    go(send(g, g_x, 0, w))
    go(send(g, g_up, 1, w))
    go(send(g, g_down, 2, w))
    go(send(g, g_core, 7, w))

    def source_of(d):
        index = jnp.int32(0)
        for j in range(N_DP):
            index = index + jnp.where(slot_dest[j] == d, j, 0)
        return jnp.minimum(index, N_DP - 1)

    def post(i, carry):
        d = (p + i) % N_DP
        outgoing[i] = frames[source_of(d)]
        remote(outgoing.at[i], pool.at[p], a2a_send.at[i - 1], a2a_recv.at[i - 1], (d, g)).start()
        return carry

    lax.fori_loop(1, N_DP, post, 0)
    outgoing[0] = frames[source_of(p)]
    own_frames = pltpu.make_async_copy(outgoing.at[0], pool.at[p], own_sems.at[1])
    own_frames.start()

    def arrived(block, slot):
        remote(full.at[block], full.at[block], w_send.at[slot], w_recv.at[slot], (p, g_x)).wait_recv()

    arrived(g_x, 0)
    go(send(g_x, g_up, 3))
    go(send(g_x, g_down, 4))
    go(send(g_x, g_core, 8))
    b = shard_index(x_lo, down, core)
    arrived(b, 1)
    go(send(b, g_up, 5))
    go(send(b, g_core, 9))
    b = shard_index(x_lo, up, core)
    arrived(b, 2)
    go(send(b, g_core, 10))
    b = shard_index(1 - x_lo, up, core)
    arrived(b, 4)
    go(send(b, g_down, 6))
    go(send(b, g_core, 11))
    b = shard_index(1 - x_lo, down, core)
    arrived(b, 3)
    go(send(b, g_core, 12))
    b = shard_index(x_lo, across, core)
    arrived(b, 5)
    go(send(b, g_core, 13))
    b = shard_index(1 - x_lo, across, core)
    arrived(b, 6)
    go(send(b, g_core, 14))
    other = 1 - core
    theirs = [
        (x_lo, y, 7), (1 - x_lo, y, 8), (x_lo, down, 9), (x_lo, up, 10),
        (1 - x_lo, up, 11), (1 - x_lo, down, 12), (x_lo, across, 13), (1 - x_lo, across, 14),
    ]
    for bx, by, slot in theirs:
        arrived(shard_index(bx, by, other), slot)

    def collect(i, carry):
        s = (p + N_DP - i) % N_DP
        copy = remote(outgoing.at[i], pool.at[s], a2a_send.at[i - 1], a2a_recv.at[i - 1], (s, g))
        copy.wait_recv()
        copy.wait_send()
        return carry

    lax.fori_loop(1, N_DP, collect, 0)
    for copy in sent:
        copy.wait_send()
    own_frames.wait()
    own_w.wait()


def exchange(frames, slot_dest, w):
    slots, slot_len, width = frames.shape
    rows, cols = w.shape
    return pl.pallas_call(
        exchange_kernel,
        out_shape=(
            jax.ShapeDtypeStruct((slots, slot_len, width), BF),
            jax.ShapeDtypeStruct((N_SHARD, rows, cols), BF),
        ),
        in_specs=[
            pl.BlockSpec(memory_space=pltpu.VMEM),
            pl.BlockSpec(memory_space=pltpu.SMEM),
            pl.BlockSpec(memory_space=pl.ANY),
        ],
        out_specs=(pl.BlockSpec(memory_space=pl.ANY), pl.BlockSpec(memory_space=pl.ANY)),
        scratch_shapes=[
            pltpu.VMEM((slots, slot_len, width), BF),
            pltpu.SemaphoreType.DMA((2,)),
            pltpu.SemaphoreType.DMA((N_DP - 1,)),
            pltpu.SemaphoreType.DMA((N_DP - 1,)),
            pltpu.SemaphoreType.DMA((15,)),
            pltpu.SemaphoreType.DMA((15,)),
        ],
        compiler_params=pltpu.CompilerParams(
            collective_id=0, has_side_effects=True, vmem_limit_bytes=32 * 1024 * 1024
        ),
        name="exchange",
    )(frames, slot_dest, w)


ROWS = 384
WIDTH = 1536
TAPS = 31
REACH = 15
PAD = 16
LANES = 128
BLOCKS = WIDTH // LANES
TILE = 256
GROUP = 48
STEP = 32


def sigmoid(v):
    return 1.0 / (1.0 + jnp.exp(-v))


def dot(a, b):
    return lax.dot_general(a, b, (((1,), (0,)), ((), ())), preferred_element_type=F32)


def dot_t(a, b):
    return lax.dot_general(a, b, (((1,), (1,)), ((), ())), preferred_element_type=F32)


def fold(v):
    total = v[0:8]
    for q in range(1, v.shape[0] // 8):
        total = total + v[q * 8 : (q + 1) * 8]
    return total


def row_mean(blocks):
    total = blocks[0]
    for b in blocks[1:]:
        total = total + b
    return jnp.sum(total, axis=1, keepdims=True) * (1.0 / WIDTH)


def lanes(b):
    return pl.ds(b * LANES if isinstance(b, int) else pl.multiple_of(b * LANES, LANES), LANES)


def load_inputs(lengths, offsets, pool, gain1, r):
    slot_len = pool.shape[0] // N_DP
    rows = lax.broadcasted_iota(jnp.int32, (ROWS, LANES), 0)
    pick = jnp.zeros((ROWS, LANES), jnp.int32)
    behind = jnp.zeros((ROWS, LANES), jnp.int32)
    ahead = jnp.zeros((ROWS, LANES), jnp.int32)
    for s in range(N_DP):
        begin = offsets[s]
        end = begin + lengths[s]
        inside = (rows >= begin) & (rows < end)
        pick = jnp.where(inside, rows - begin + s * slot_len, pick)
        behind = jnp.where(inside, rows - begin, behind)
        ahead = jnp.where(inside, end - 1 - rows, ahead)
    r["behind"][...] = behind
    r["ahead"][...] = ahead
    lane = lax.broadcasted_iota(jnp.int32, (ROWS, LANES), 1)
    for t in range(pool.shape[0] // LANES):
        r["chosen"][:, lanes(t)] = (pick == lane + t * LANES).astype(F32).astype(BF)

    def gather(t, carry):
        cols = pl.ds(pl.multiple_of(t * TILE, TILE), TILE)
        r["unit_in"][:, cols] = dot(r["chosen"][...], pool[:, cols])
        return carry

    lax.fori_loop(0, WIDTH // TILE, gather, 0)

    def norm(i, carry):
        rows = pl.ds(pl.multiple_of(i * STEP, STEP), STEP)
        x = [r["unit_in"][rows, lanes(b)] for b in range(BLOCKS)]
        mean = row_mean(x)
        x = [v - mean for v in x]
        inverse = lax.rsqrt(row_mean([v * v for v in x]) + EPSILON)
        r["inv_in"][rows, :] = jnp.broadcast_to(inverse, (STEP, LANES))
        for b in range(BLOCKS):
            unit = x[b] * inverse
            r["unit_in"][rows, lanes(b)] = unit
            r["normed"][rows, lanes(b)] = (unit * gain1[lanes(b)].reshape(1, LANES)).astype(BF)
        return carry

    lax.fori_loop(0, ROWS // STEP, norm, 0)


def transpose_normed(r):
    for b in range(BLOCKS):
        r["normed_t"][lanes(b), :] = r["normed"][:, lanes(b)].T


def project(w, wait_tile, r):
    def tile(t, carry):
        wait_tile(t)
        cols = pl.ds(pl.multiple_of(t * TILE, TILE), TILE)
        gates = pl.ds(pl.multiple_of(t * TILE + WIDTH, TILE), TILE)
        linear = dot(r["normed"][...], w[:, cols])
        sig = sigmoid(dot(r["normed"][...], w[:, gates]))
        r["linear"][:, cols] = linear
        r["sig"][:, cols] = sig
        gated = (linear * sig).astype(BF).astype(F32)
        for j in range(TILE // LANES):
            r["gated"][t * (TILE // LANES) + j, PAD : PAD + ROWS, :] = gated[:, j * LANES : (j + 1) * LANES]
        return carry

    lax.fori_loop(0, WIDTH // TILE, tile, 0)


def tap_mask(behind, ahead, shift):
    return ahead >= shift if shift > 0 else behind >= -shift


def convolve(w_depth, r):
    def pair(c, carry):
        for g in range(ROWS // GROUP):
            begin = g * GROUP
            behind = r["behind"][begin : begin + GROUP, :]
            ahead = r["ahead"][begin : begin + GROUP, :]
            total = [jnp.zeros((GROUP, LANES), F32)] * 2
            for k in range(TAPS):
                shift = k - REACH
                same = tap_mask(behind, ahead, shift)
                for j in range(2):
                    b = c * 2 + j
                    x = r["gated"][b, PAD + begin + shift : PAD + begin + shift + GROUP, :]
                    if shift != 0:
                        x = jnp.where(same, x, 0.0)
                    total[j] = total[j] + x * w_depth[k : k + 1, lanes(b)]
            for j in range(2):
                r["conv"][c * 2 + j, PAD + begin : PAD + begin + GROUP, :] = total[j]
        return carry

    lax.fori_loop(0, BLOCKS // 2, pair, 0)


def finish_forward(gain2, cotangent, output, r):
    r["gain2_sum"][...] = jnp.zeros_like(r["gain2_sum"])

    def row_step(i, carry):
        rows = pl.ds(pl.multiple_of(i * STEP, STEP), STEP)
        held = pl.ds(pl.multiple_of(i * STEP + PAD, 16), STEP)
        x = [r["conv"][b, held, :] for b in range(BLOCKS)]
        mean = row_mean(x)
        x = [v - mean for v in x]
        inverse = lax.rsqrt(row_mean([v * v for v in x]) + EPSILON)
        units, grads = [], []
        for b in range(BLOCKS):
            unit = x[b] * inverse
            gain = gain2[lanes(b)].reshape(1, LANES)
            scaled = unit * gain
            sig = sigmoid(scaled)
            output[rows, lanes(b)] = (scaled * sig).astype(BF)
            grad = cotangent[rows, lanes(b)].astype(F32) * sig * (1.0 + scaled * (1.0 - sig))
            both = grad * unit
            r["gain2_sum"][b] = r["gain2_sum"][b] + fold(both)
            units.append(unit)
            grads.append(grad * gain)
        first = row_mean(grads)
        second = row_mean([q * u for q, u in zip(grads, units)])
        for b in range(BLOCKS):
            r["conv"][b, held, :] = inverse * (grads[b] - first - units[b] * second)
        return carry

    lax.fori_loop(0, ROWS // STEP, row_step, 0)


def back_convolve(chunk, w_depth, small, r):
    def pair(c, carry):
        first = chunk * (HALF // LANES) + c * 2
        r["tap_sum"][...] = jnp.zeros_like(r["tap_sum"])
        for g in range(ROWS // GROUP):
            begin = g * GROUP
            rows = slice(begin, begin + GROUP)
            behind = r["behind"][rows, :]
            ahead = r["ahead"][rows, :]
            total = [jnp.zeros((GROUP, LANES), F32)] * 2
            gated = [r["gated"][first + j, PAD + begin : PAD + begin + GROUP, :] for j in range(2)]
            for k in range(TAPS):
                shift = REACH - k
                same = tap_mask(behind, ahead, shift)
                for j in range(2):
                    x = r["conv"][first + j, PAD + begin + shift : PAD + begin + shift + GROUP, :]
                    if shift != 0:
                        x = jnp.where(same, x, 0.0)
                    total[j] = total[j] + x * w_depth[k : k + 1, lanes(first + j)]
                    product = x * gated[j]
                    r["tap_sum"][j, k] = r["tap_sum"][j, k] + fold(product)
            for j in range(2):
                at = pl.multiple_of((first + j) * LANES, LANES)
                linear = r["linear"][rows, pl.ds(at, LANES)]
                sig = r["sig"][rows, pl.ds(at, LANES)]
                grad = total[j] * sig
                r["grad_pre"][rows, pl.ds(at, LANES)] = grad.astype(BF)
                r["grad_pre"][rows, pl.ds(at + WIDTH, LANES)] = (grad * linear * (1.0 - sig)).astype(BF)
        for j in range(2):
            at = pl.multiple_of((first + j) * LANES, LANES)
            small[0:TAPS, pl.ds(at, LANES)] = jnp.sum(r["tap_sum"][j], axis=1)
        return carry

    lax.fori_loop(0, HALF // LANES // 2, pair, 0)


def weight_term(chunk, part, r):
    def tile(i, carry):
        rows = pl.ds(pl.multiple_of(i * 384, 384), 384)
        for h in range(2):
            cols = pl.ds(h * WIDTH + chunk * HALF, HALF)
            value = dot(r["normed_t"][rows, :], r["grad_pre"][:, cols]).astype(BF)
            for q in range(4):
                part[i // 2, (i % 2) * 2 + q // 2, q % 2, :, h * HALF : (h + 1) * HALF] = value[q * 96 : (q + 1) * 96]
        return carry

    lax.fori_loop(0, 4, tile, 0)


def back_project(w, r):
    def tile(t, carry):
        cols = pl.ds(pl.multiple_of(t * TILE, TILE), TILE)
        r["linear"][:, cols] = dot_t(r["grad_pre"][...], w[cols, :])
        return carry

    lax.fori_loop(0, WIDTH // TILE, tile, 0)


def finish_back(gain1, grad_input, small, r):
    r["gain1_sum"][...] = jnp.zeros_like(r["gain1_sum"])

    def row_step(i, carry):
        rows = pl.ds(pl.multiple_of(i * STEP, STEP), STEP)
        inverse = r["inv_in"][rows, :]
        units = [r["unit_in"][rows, lanes(b)] for b in range(BLOCKS)]
        grads = [r["linear"][rows, lanes(b)] for b in range(BLOCKS)]
        for b in range(BLOCKS):
            both = grads[b] * units[b]
            r["gain1_sum"][b] = r["gain1_sum"][b] + fold(both)
        grads = [grads[b] * gain1[lanes(b)].reshape(1, LANES) for b in range(BLOCKS)]
        first = row_mean(grads)
        second = row_mean([q * u for q, u in zip(grads, units)])
        for b in range(BLOCKS):
            grad_input[rows, lanes(b)] = (inverse * (grads[b] - first - units[b] * second)).astype(BF)
        return carry

    lax.fori_loop(0, ROWS // STEP, row_step, 0)
    for b in range(BLOCKS):
        small[TAPS : TAPS + 1, lanes(b)] = jnp.sum(r["gain1_sum"][b], axis=0, keepdims=True)
        small[TAPS + 1 : TAPS + 2, lanes(b)] = jnp.sum(r["gain2_sum"][b], axis=0, keepdims=True)
    small[TAPS + 2 : SMALL_ROWS, :] = jnp.zeros((SMALL_ROWS - TAPS - 2, WIDTH), F32)


WORK = (
    ("behind", (ROWS, LANES), jnp.int32),
    ("ahead", (ROWS, LANES), jnp.int32),
    ("chosen", (ROWS, 640), BF),
    ("unit_in", (ROWS, WIDTH), F32),
    ("inv_in", (ROWS, LANES), F32),
    ("normed", (ROWS, WIDTH), BF),
    ("normed_t", (WIDTH, ROWS), BF),
    ("linear", (ROWS, WIDTH), F32),
    ("sig", (ROWS, WIDTH), F32),
    ("gated", (BLOCKS, PAD + ROWS + PAD, LANES), F32),
    ("conv", (BLOCKS, PAD + ROWS + PAD, LANES), F32),
    ("gain1_sum", (BLOCKS, 8, LANES), F32),
    ("gain2_sum", (BLOCKS, 8, LANES), F32),
    ("tap_sum", (2, TAPS, 8, LANES), F32),
    ("grad_pre", (ROWS, 2 * WIDTH), BF),
)


def forward(lengths, offsets, pool, w_hbm, gain1, w_depth, gain2, cotangent, output, w, w_sems, r):
    def copy_w(t, h):
        cols = pl.ds(pl.multiple_of(t * TILE + h * WIDTH, TILE), TILE)
        return pltpu.make_async_copy(w_hbm.at[:, cols], w.at[:, cols], w_sems.at[h, t])

    for t in range(WIDTH // TILE):
        for h in range(2):
            copy_w(t, h).start()

    def wait_tile(t):
        for h in range(2):
            copy_w(t, h).wait()

    for name in ("gated", "conv"):
        r[name][:, 0:PAD, :] = jnp.zeros((BLOCKS, PAD, LANES), F32)
        r[name][:, PAD + ROWS :, :] = jnp.zeros((BLOCKS, PAD, LANES), F32)
    load_inputs(lengths, offsets, pool, gain1, r)
    project(w, wait_tile, r)
    convolve(w_depth, r)
    finish_forward(gain2, cotangent, output, r)
    transpose_normed(r)


def add_blocks(dst, src, count, cols):
    def step(i, carry):
        block, row = i // 2, pl.multiple_of((i % 2) * 48, 48)
        d, s = dst(block), src(block)
        value = d[pl.ds(row, 48), cols].astype(F32) + s[pl.ds(row, 48), :].astype(F32)
        d[pl.ds(row, 48), cols] = value.astype(BF)
        return carry

    lax.fori_loop(0, count * 2, step, 0)


X_FIRST = (False, True, False)


def module_kernel(
    lengths, offsets, pool, w_hbm, gain1, w_depth, gain2, cotangent,
    output, grad_input, out, small_out,
    w, w_sems, small, part, rx0, rx1, rx2, rx3, rx3_all, rx4, red, fin, rxs, rxd, small_fin,
    s0, r0, s1, r1, s2, r2, s3, r3, s4, r4, s5, r5, st1, rt1, st2, rt2, st3, rt3,
    *work
):
    r = {name: ref for (name, _, _), ref in zip(WORK, work)}
    p, g = lax.axis_index("dp"), lax.axis_index("shard")
    x_lo, y, core = g // 8, (g // 2) % 4, g % 2
    mates = (y + 1 - 2 * (y % 2), 3 - y)
    scale = 1.0 / (N_DP * N_SHARD)

    barrier = pltpu.get_barrier_semaphore()

    def greet(i, carry):
        signal(barrier, ((p + i) % N_DP, g))
        signal(barrier, (p, (g + i) % N_SHARD))
        return carry

    lax.fori_loop(1, 16, greet, 0)

    def core_copy(k):
        return remote(
            part.at[k, :, :, 1 - core], rx0.at[k], s0.at[k], r0.at[k], (p, shard_index(x_lo, y, 1 - core))
        )

    def finish_core(k):
        core_copy(k).wait_recv()
        add_blocks(
            lambda i: part.at[k, i // 4, i % 4, core], lambda i: rx0.at[k, i // 4, i % 4], 8, slice(None)
        )

    def cols(h):
        return pl.ds(HALF * h, HALF)

    def wide(k):
        return 1 if X_FIRST[k] else 2

    def first_x(k, i):
        return x_lo if X_FIRST[k] else i

    def y_block(k, block, h):
        if X_FIRST[k]:
            return part.at[k, pl.ds(x_lo, 1), block, core, :, cols(h)]
        return part.at[k, :, block, core, :, cols(h)]

    def y1_copy(k, h, j):
        q = mates[h]
        after = 3 - q if h == 0 else q + 1 - 2 * (q % 2)
        return remote(
            y_block(k, q if j == 0 else after, h), rx1.at[k, h, j, pl.ds(0, wide(k))],
            s1.at[k, h, j], r1.at[k, h, j], (p, shard_index(x_lo, q, core)),
        )

    def start_y1(k):
        for j in (1, 0):
            for h in range(2):
                y1_copy(k, h, j).start()

    def y2_copy(k, h):
        q = mates[1 - h]
        return remote(
            y_block(k, q, h), rx2.at[k, h, pl.ds(0, wide(k))], s2.at[k, h], r2.at[k, h],
            (p, shard_index(x_lo, q, core)),
        )

    def turn_y(k):
        for h in range(2):
            y1_copy(k, h, 1).wait_recv()
            add_blocks(
                lambda i: part.at[k, first_x(k, i), mates[1 - h], core],
                lambda i: rx1.at[k, h, 1, i], wide(k), cols(h),
            )
            y2_copy(k, h).start()
        for h in range(2):
            y1_copy(k, h, 0).wait_recv()
            add_blocks(
                lambda i: part.at[k, first_x(k, i), y, core], lambda i: rx1.at[k, h, 0, i], wide(k), cols(h)
            )

    def finish_y(k):
        for h in range(2):
            y2_copy(k, h).wait_recv()
            add_blocks(
                lambda i: part.at[k, first_x(k, i), y, core], lambda i: rx2.at[k, h, i], wide(k), cols(h)
            )

    def x_copy(k):
        peer = (p, shard_index(1 - x_lo, y, core))
        if X_FIRST[k]:
            return remote(part.at[k, 1 - x_lo, :, core], rx3_all, s3.at[k], r3.at[k], peer)
        return remote(part.at[k, 1 - x_lo, y, core], rx3.at[k], s3.at[k], r3.at[k], peer)

    def finish_x(k):
        x_copy(k).wait_recv()
        if X_FIRST[k]:
            add_blocks(lambda i: part.at[k, x_lo, i, core], lambda i: rx3_all.at[i], 4, slice(None))
        else:
            add_blocks(lambda i: part.at[k, x_lo, y, core], lambda i: rx3.at[k], 1, slice(None))

    def at_piece(ref, d, base):
        return ref.at[
            pl.ds(pl.multiple_of((d % 2) * 48, 48), 48), pl.ds(pl.multiple_of(base + (d // 2) * 128, 128), 128)
        ]

    def piece_copy(k, i):
        d = (p + i) % N_DP
        return remote(
            at_piece(part.at[k, x_lo, y, core], d, 0), rx4.at[k, i - 1], s4.at[k, i - 1], r4.at[k, i - 1], (d, g)
        )

    def sum_copy(k, i, sender):
        d = (p + i) % N_DP
        return remote(red.at[k], at_piece(fin, sender, CHUNK * k), s5.at[k, i - 1], r5.at[k, i - 1], (d, g))

    def each(count, do):
        def step(i, carry):
            do(i)
            return carry

        lax.fori_loop(1, count, step, 0)

    def start_pieces(k):
        each(N_DP, lambda i: piece_copy(k, i).start())

    def turn_pieces(k):
        each(N_DP, lambda i: piece_copy(k, i).wait_recv())
        total = at_piece(part.at[k, x_lo, y, core], p, 0)[...].astype(F32)
        for i in range(N_DP - 1):
            total = total + rx4[k, i].astype(F32)
        total = total.astype(BF)
        red[k] = total
        at_piece(fin, p, CHUNK * k)[...] = total
        each(N_DP, lambda i: sum_copy(k, i, p).start())

    def finish_pieces(k):
        each(N_DP, lambda i: sum_copy(k, i, (p + N_DP - i) % N_DP).wait_recv())

        def widen(i, carry):
            rows = pl.ds(pl.multiple_of(i * 48, 48), 48)
            for h in range(2):
                out[rows, pl.ds(h * WIDTH + HALF * k, HALF)] = (
                    fin[rows, pl.ds(CHUNK * k + HALF * h, HALF)].astype(F32) * scale
                )
            return carry

        lax.fori_loop(0, 2, widen, 0)

    def column(j):
        return pl.ds(pl.multiple_of(j * LANES, LANES), LANES)

    def small_copy(j):
        return remote(small.at[:, column(j)], rxs.at[g], st1.at[j], rt1.at[g], (p, j))

    def each_owner(do):
        def step(j, carry):
            @pl.when(j != g)
            def _():
                do(j)

            return carry

        lax.fori_loop(0, SMALL_OWNERS, step, 0)

    def small_sum_copy(i):
        return remote(rxd.at[p], rxd.at[p], st2.at[i - 1], rt2.at[p], ((p + i) % N_DP, g))

    def small_final_copy(i):
        return remote(
            small_fin.at[:, column(g)], small_fin.at[:, column(g)], st3.at[i - 1], rt3.at[g],
            (p, (g + i) % N_SHARD),
        )

    def add_small_shard():
        @pl.when(g < SMALL_OWNERS)
        def _():
            def take(i):
                s = (g + i) % N_SHARD
                remote(small.at[:, column(0)], rxs.at[s], st1.at[0], rt1.at[s], (p, s)).wait_recv()

            each(N_SHARD, take)
            rxs[g] = small[:, column(g)]
            total = rxs[0]
            for s in range(1, N_SHARD):
                total = total + rxs[s]
            rxd[p] = total
            each(N_DP, lambda i: small_sum_copy(i).start())

    def add_small_dp():
        @pl.when(g < SMALL_OWNERS)
        def _():
            def take(i):
                s = (p + i) % N_DP
                remote(rxd.at[s], rxd.at[s], st2.at[0], rt2.at[s], (s, g)).wait_recv()

            each(N_DP, take)
            total = rxd[0]
            for s in range(1, N_DP):
                total = total + rxd[s]
            small_fin[:, column(g)] = total
            each(N_SHARD, lambda i: small_final_copy(i).start())

    forward(lengths, offsets, pool, w_hbm, gain1, w_depth, gain2, cotangent, output, w, w_sems, r)
    pl.semaphore_wait(barrier, 30)
    for k in range(CHUNKS):
        back_convolve(k, w_depth, small, r)
        weight_term(k, part.at[k], r)
        core_copy(k).start()
        if k == 1:
            finish_core(0)
            start_y1(0)
    finish_core(1)
    x_copy(1).start()
    back_project(w, r)
    finish_core(2)
    start_y1(2)
    turn_y(0)
    finish_back(gain1, grad_input, small, r)
    each_owner(lambda j: small_copy(j).start())
    finish_y(0)
    x_copy(0).start()
    turn_y(2)
    finish_x(1)
    start_y1(1)
    finish_x(0)
    start_pieces(0)
    add_small_shard()
    finish_y(2)
    x_copy(2).start()
    turn_y(1)
    turn_pieces(0)
    finish_x(2)
    start_pieces(2)
    finish_y(1)
    start_pieces(1)
    add_small_dp()
    turn_pieces(2)
    turn_pieces(1)

    def take_final(j):
        remote(
            small_fin.at[:, column(j)], small_fin.at[:, column(j)], st3.at[0], rt3.at[j], (p, j)
        ).wait_recv()

    each_owner(take_final)
    small_out[...] = small_fin[...] * scale
    for k in (0, 2, 1):
        finish_pieces(k)

    for k in range(CHUNKS):
        core_copy(k).wait_send()
        x_copy(k).wait_send()
        for h in range(2):
            y1_copy(k, h, 0).wait_send()
            y1_copy(k, h, 1).wait_send()
            y2_copy(k, h).wait_send()

        def sent(i):
            piece_copy(k, i).wait_send()
            sum_copy(k, i, p).wait_send()

        each(N_DP, sent)
    each_owner(lambda j: small_copy(j).wait_send())

    @pl.when(g < SMALL_OWNERS)
    def _():
        def sent(i):
            small_sum_copy(i).wait_send()
            small_final_copy(i).wait_send()

        each(16, sent)


def module(lengths, offsets, pool, full, gain1, w_depth, gain2, cotangent):
    vmem = pl.BlockSpec(memory_space=pltpu.VMEM)
    smem = pl.BlockSpec(memory_space=pltpu.SMEM)
    block = WIDTH // N_SHARD
    dma = pltpu.SemaphoreType.DMA
    return pl.pallas_call(
        module_kernel,
        out_shape=(
            jax.ShapeDtypeStruct((ROWS, WIDTH), BF),
            jax.ShapeDtypeStruct((ROWS, WIDTH), BF),
            jax.ShapeDtypeStruct((block, 2 * WIDTH), F32),
            jax.ShapeDtypeStruct((SMALL_ROWS, WIDTH), F32),
        ),
        in_specs=[smem, smem, vmem, pl.BlockSpec(memory_space=pl.ANY), vmem, vmem, vmem, vmem],
        out_specs=(vmem,) * 4,
        scratch_shapes=[
            pltpu.VMEM((WIDTH, 2 * WIDTH), BF),
            dma((2, WIDTH // TILE)),
            pltpu.VMEM((SMALL_ROWS, WIDTH), F32),
            pltpu.VMEM((CHUNKS, 2, 4, 2, block, CHUNK), BF),
            pltpu.VMEM((CHUNKS, 2, 4, block, CHUNK), BF),
            pltpu.VMEM((CHUNKS, 2, 2, 2, block, HALF), BF),
            pltpu.VMEM((CHUNKS, 2, 2, block, HALF), BF),
            pltpu.VMEM((CHUNKS, block, CHUNK), BF),
            pltpu.VMEM((4, block, CHUNK), BF),
            pltpu.VMEM((CHUNKS, N_DP - 1, block // 2, 128), BF),
            pltpu.VMEM((CHUNKS, block // 2, 128), BF),
            pltpu.VMEM((block, 2 * WIDTH), BF),
            pltpu.VMEM((N_SHARD, SMALL_ROWS, 128), F32),
            pltpu.VMEM((N_DP, SMALL_ROWS, 128), F32),
            pltpu.VMEM((SMALL_ROWS, WIDTH), F32),
            dma((CHUNKS,)), dma((CHUNKS,)),
            dma((CHUNKS, 2, 2)), dma((CHUNKS, 2, 2)),
            dma((CHUNKS, 2)), dma((CHUNKS, 2)),
            dma((CHUNKS,)), dma((CHUNKS,)),
            dma((CHUNKS, N_DP - 1)), dma((CHUNKS, N_DP - 1)),
            dma((CHUNKS, N_DP - 1)), dma((CHUNKS, N_DP - 1)),
            dma((SMALL_OWNERS,)), dma((N_SHARD,)),
            dma((N_DP - 1,)), dma((N_DP,)),
            dma((N_SHARD - 1,)), dma((SMALL_OWNERS,)),
            *[pltpu.VMEM(shape, dtype) for _, shape, dtype in WORK],
        ],
        compiler_params=pltpu.CompilerParams(
            collective_id=1, has_side_effects=True, vmem_limit_bytes=60 * 1024 * 1024
        ),
        name="module",
    )(lengths, offsets, pool, full, gain1, w_depth, gain2, cotangent)


def body(frames, slot_dest, recv_length, recv_offset, gain1, w_in, w_depth, gain2, cotangent):
    model_width = frames.shape[2]
    taps = w_depth.shape[0]
    pool, full = exchange(frames, slot_dest, w_in)
    output, grad_input, grad_w, small_sum = module(
        recv_length, recv_offset, pool.reshape(-1, model_width), full.reshape(model_width, 2 * model_width),
        gain1, w_depth, gain2, cotangent,
    )
    return (output, grad_input, grad_w, small_sum[:taps], small_sum[taps], small_sum[taps + 1])


def solution(mesh):
    in_specs = (
        P(("dp", "shard"), None, None),
        P(("dp", "shard")),
        P(("dp", "shard")),
        P(("dp", "shard")),
        P(),
        P("shard", None),
        P(),
        P(),
        P(("dp", "shard"), None),
    )
    out_specs = (
        P(("dp", "shard"), None),
        P(("dp", "shard"), None),
        P("shard", None),
        P(),
        P(),
        P(),
    )
    return jax.shard_map(body, mesh=mesh, in_specs=in_specs, out_specs=out_specs, check_vma=False)
```

time: 238 us -> 211 us (0.89)
  Pallas kernels: 217 us -> 194 us
    pallas_call x1 -> x0, Pallas kernels: 85.5 us -> none  [reduce_gradients(): pl.pallas_call(reduce_kernel, out_shape=(jax.ShapeDtypeStruct((block, col...]
    pallas_call x1, Pallas kernels: 68.6 us -> 131 us  [module(): pl.pallas_call(module_kernel, out_shape=(jax.ShapeDtypeStruct((ROWS, WIDT...]
    broadcast_in_dim x2 -> x0, local copies, waits for them, and re-layouts: 2.65 us -> none  [the longest x1 1.36 us: body(): gain1[None]]
    unnamed x15 -> x17, local copies, waits for them, and re-layouts: 12.7 us -> 13.3 us
where the time goes in v3:
time: 211 us
  Pallas kernels  194 us (92%)
  local copies, waits for them, and re-layouts  16.4 us (8%)
    pallas_call x1, Pallas kernels, module(): pl.pallas_call(module_kernel, out_shape=(jax.ShapeDtypeStruct((ROWS, WIDT...  131 us
    pallas_call x1, Pallas kernels, exchange(): pl.pallas_call(exchange_kernel, out_shape=(jax.ShapeDtypeStruct((slots, s...  63.2 us
    unnamed x17, local copies, waits for them, and re-layouts  13.3 us

profile of v3, /device:TPU:6, one launch (start us, length us, event | category | flops | bytes accessed | tf_op | source)
XLA Modules:
  0.0 211.0 jit_solution(14134427767523770073)
XLA Ops:
  0.6 0.0 copy-start.2
  0.6 1.5 copy-done.2
  2.2 0.0 copy-start.3
  2.2 1.1 copy-done.3
  3.2 0.0 copy-start.4
  3.2 0.7 copy-done.4
  3.9 63.2 %exchange.1 = (bf16[16,40,1536]{2,1,0:T(8,128)(2,1)S(1)}, bf16[16,96,3072]{2,1,0:T(8,128)(2,1)S(1)}) custom-call(bf16[16,40,1536]{2,1,0:T(8,128)(2,1)S(1)} %copy-done.2, s32[16]{0:T(128)S(1)} %copy-done.4, bf16[96,3072]{1,0:T(8,128)(2,1)S(1)} %copy-done.3), custom_call_target="tpu_custom_call" | custom-call | tf_op jit(solution)/shard_map/exchange/pallas_call | solution.py:146
  67.1 0.0 copy-start
  67.1 3.6 %copy-done = bf16[16,96,3072]{2,1,0:T(8,128)(2,1)} copy-done((bf16[16,96,3072]{2,1,0:T(8,128)(2,1)}, bf16[16,96,3072]{2,1,0:T(8,128)(2,1)S(1)}, u32[]{:S(2)}) %copy-start) | copy-done | bytes 9437208
  70.7 0.0 copy-start.1
  70.7 1.3 copy-done.1
  72.0 130.8 %module.1 = (bf16[384,1536]{1,0:T(8,128)(2,1)}, bf16[384,1536]{1,0:T(8,128)(2,1)}, f32[96,3072]{1,0:T(8,128)}, f32[40,1536]{1,0:T(8,128)}) custom-call(s32[16]{0:T(128)} %lengths.1, s32[16]{0:T(128)} %offsets.1, bf16[640,1536]{1,0:T(8,128)(2,1)} %bitcast.3, bf16[1536,3072]{1,0:T(8,128)(2,1)} %bitcast.2, f32[1536]{0:T(1024)} %gain1.1, f32[31,1536]{1,0:T(8,128)} %w_depth.1, ...), custom_call_target="tpu_custom_call" | custom-call | tf_op jit(solution)/shard_map/module/pallas_call | solution.py:755
  202.7 1.5 slice_reduce_fusion
  204.2 1.6 slice.9
  205.8 0.0 copy-start.6
  205.8 2.5 %copy.18 = bf16[384,1536]{1,0:T(8,128)(2,1)} copy(bf16[384,1536]{1,0:T(8,128)(2,1)} %get-tuple-element.26) | data formatting | bytes 2359296
  208.3 0.0 copy-done.6
  208.3 0.0 copy-start.5
  208.3 1.0 copy.19
  209.3 0.7 copy-done.5
  210.0 1.0 copy.20
Async XLA Ops:
  0.6 1.5 copy-start.2
  2.2 1.1 copy-start.3
  3.2 0.7 copy-start.4
  67.1 3.6 %copy-start = (bf16[16,96,3072]{2,1,0:T(8,128)(2,1)}, bf16[16,96,3072]{2,1,0:T(8,128)(2,1)S(1)}, u32[]{:S(2)}) copy-start(bf16[16,96,3072]{2,1,0:T(8,128)(2,1)S(1)} %get-tuple-element.13) | copy-start | bytes 28311556
  70.7 1.3 copy-start.1
  205.8 2.5 %copy-start.6 = (bf16[384,1536]{1,0:T(8,128)(2,1)S(1)}, bf16[384,1536]{1,0:T(8,128)(2,1)}, u32[]{:S(2)}) copy-start(bf16[384,1536]{1,0:T(8,128)(2,1)} %get-tuple-element.27) | copy-start | bytes 3538948
  208.3 1.7 copy-start.5

commit v4 on v3

--- a/solution.py
+++ b/solution.py
@@ -33,9 +33,14 @@
     )
 
 
-def exchange_kernel(
-    frames, slot_dest, w, pool, full, outgoing, own_sems, a2a_send, a2a_recv, w_send, w_recv
-):
+def source_of(slot_dest, d):
+    index = jnp.int32(0)
+    for j in range(N_DP):
+        index = index + jnp.where(slot_dest[j] == d, j, 0)
+    return jnp.minimum(index, N_DP - 1)
+
+
+def exchange(frames, slot_dest, w_own, pool, w, outgoing, own_sem, a2a_send, a2a_recv, w_send, w_recv, between):
     p, g = lax.axis_index("dp"), lax.axis_index("shard")
     x_lo, y, core = g // 8, (g // 2) % 4, g % 2
     up, down, across = (y + 1) % 4, (y + 3) % 4, (y + 2) % 4
@@ -43,24 +48,14 @@
     g_up = shard_index(x_lo, up, core)
     g_down = shard_index(x_lo, down, core)
     g_core = shard_index(x_lo, y, 1 - core)
-
-    barrier = pltpu.get_barrier_semaphore()
-
-    def greet(i, carry):
-        signal(barrier, ((p + i) % N_DP, g))
-        return carry
-
-    lax.fori_loop(1, N_DP, greet, 0)
-    for peer in (g_x, g_up, g_down, g_core):
-        signal(barrier, (p, peer))
-
-    own_w = pltpu.make_async_copy(w, full.at[g], own_sems.at[0])
-    own_w.start()
-    pl.semaphore_wait(barrier, N_DP - 1 + 4)
+    depth = w_own.shape[0]
+
+    def rows(block):
+        return w.at[pl.ds(pl.multiple_of(block * depth, depth), depth), :]
 
     def send(block, peer, slot, src=None):
         return remote(
-            full.at[block] if src is None else src, full.at[block], w_send.at[slot], w_recv.at[slot], (p, peer)
+            rows(block) if src is None else src, rows(block), w_send.at[slot], w_recv.at[slot], (p, peer)
         )
 
     sent = []
@@ -69,30 +64,27 @@
         copy.start()
         sent.append(copy)
 
-    go(send(g, g_x, 0, w))
-    go(send(g, g_up, 1, w))
-    go(send(g, g_down, 2, w))
-    go(send(g, g_core, 7, w))
-
-    def source_of(d):
-        index = jnp.int32(0)
-        for j in range(N_DP):
-            index = index + jnp.where(slot_dest[j] == d, j, 0)
-        return jnp.minimum(index, N_DP - 1)
+    go(send(g, g_up, 1, w_own))
+    go(send(g, g_down, 2, w_own))
+    go(send(g, g_x, 0, w_own))
 
     def post(i, carry):
-        d = (p + i) % N_DP
-        outgoing[i] = frames[source_of(d)]
-        remote(outgoing.at[i], pool.at[p], a2a_send.at[i - 1], a2a_recv.at[i - 1], (d, g)).start()
-        return carry
-
-    lax.fori_loop(1, N_DP, post, 0)
-    outgoing[0] = frames[source_of(p)]
-    own_frames = pltpu.make_async_copy(outgoing.at[0], pool.at[p], own_sems.at[1])
-    own_frames.start()
+        d = (p + i + 6) % N_DP
+        j = jnp.where(i + 6 < N_DP, i + 6, i + 6 - N_DP)
+        outgoing[j] = frames[source_of(slot_dest, d)]
+        remote(outgoing.at[j], pool.at[p], a2a_send.at[j], a2a_recv.at[j], (d, g)).start()
+        return carry
+
+    lax.fori_loop(0, N_DP - 6, post, 0)
+    lax.fori_loop(N_DP - 5, N_DP, post, 0)
+    go(send(g, g_core, 7, w_own))
+    own_w = pltpu.make_async_copy(w_own, rows(g), own_sem)
+    own_w.start()
+    pool[p] = frames[source_of(slot_dest, p)]
+    between()
 
     def arrived(block, slot):
-        remote(full.at[block], full.at[block], w_send.at[slot], w_recv.at[slot], (p, g_x)).wait_recv()
+        remote(rows(block), rows(block), w_send.at[slot], w_recv.at[slot], (p, g_x)).wait_recv()
 
     arrived(g_x, 0)
     go(send(g_x, g_up, 3))
@@ -118,56 +110,35 @@
     b = shard_index(1 - x_lo, across, core)
     arrived(b, 6)
     go(send(b, g_core, 14))
-    other = 1 - core
-    theirs = [
-        (x_lo, y, 7), (1 - x_lo, y, 8), (x_lo, down, 9), (x_lo, up, 10),
-        (1 - x_lo, up, 11), (1 - x_lo, down, 12), (x_lo, across, 13), (1 - x_lo, across, 14),
-    ]
-    for bx, by, slot in theirs:
-        arrived(shard_index(bx, by, other), slot)
 
     def collect(i, carry):
         s = (p + N_DP - i) % N_DP
-        copy = remote(outgoing.at[i], pool.at[s], a2a_send.at[i - 1], a2a_recv.at[i - 1], (s, g))
+        copy = remote(outgoing.at[i], pool.at[s], a2a_send.at[i], a2a_recv.at[i], (s, g))
         copy.wait_recv()
-        copy.wait_send()
         return carry
 
     lax.fori_loop(1, N_DP, collect, 0)
-    for copy in sent:
-        copy.wait_send()
-    own_frames.wait()
-    own_w.wait()
-
-
-def exchange(frames, slot_dest, w):
-    slots, slot_len, width = frames.shape
-    rows, cols = w.shape
-    return pl.pallas_call(
-        exchange_kernel,
-        out_shape=(
-            jax.ShapeDtypeStruct((slots, slot_len, width), BF),
-            jax.ShapeDtypeStruct((N_SHARD, rows, cols), BF),
-        ),
-        in_specs=[
-            pl.BlockSpec(memory_space=pltpu.VMEM),
-            pl.BlockSpec(memory_space=pltpu.SMEM),
-            pl.BlockSpec(memory_space=pl.ANY),
-        ],
-        out_specs=(pl.BlockSpec(memory_space=pl.ANY), pl.BlockSpec(memory_space=pl.ANY)),
-        scratch_shapes=[
-            pltpu.VMEM((slots, slot_len, width), BF),
-            pltpu.SemaphoreType.DMA((2,)),
-            pltpu.SemaphoreType.DMA((N_DP - 1,)),
-            pltpu.SemaphoreType.DMA((N_DP - 1,)),
-            pltpu.SemaphoreType.DMA((15,)),
-            pltpu.SemaphoreType.DMA((15,)),
-        ],
-        compiler_params=pltpu.CompilerParams(
-            collective_id=0, has_side_effects=True, vmem_limit_bytes=32 * 1024 * 1024
-        ),
-        name="exchange",
-    )(frames, slot_dest, w)
+
+    def finish_weight():
+        other = 1 - core
+        theirs = [
+            (x_lo, y, 7), (1 - x_lo, y, 8), (x_lo, down, 9), (x_lo, up, 10),
+            (1 - x_lo, up, 11), (1 - x_lo, down, 12), (x_lo, across, 13), (1 - x_lo, across, 14),
+        ]
+        for bx, by, slot in theirs:
+            arrived(shard_index(bx, by, other), slot)
+        own_w.wait()
+
+    def finish_sends():
+        def collect_sent(i, carry):
+            remote(outgoing.at[i], pool.at[p], a2a_send.at[i], a2a_recv.at[i], (p, g_x)).wait_send()
+            return carry
+
+        lax.fori_loop(1, N_DP, collect_sent, 0)
+        for copy in sent:
+            copy.wait_send()
+
+    return finish_weight, finish_sends
 
 
 ROWS = 384
@@ -180,6 +151,7 @@
 TILE = 256
 GROUP = 48
 STEP = 32
+SLOT = 40
 
 
 def sigmoid(v):
@@ -212,8 +184,8 @@
     return pl.ds(b * LANES if isinstance(b, int) else pl.multiple_of(b * LANES, LANES), LANES)
 
 
-def load_inputs(lengths, offsets, pool, gain1, r):
-    slot_len = pool.shape[0] // N_DP
+def find_rows(lengths, offsets, r):
+    slot_len = SLOT
     rows = lax.broadcasted_iota(jnp.int32, (ROWS, LANES), 0)
     pick = jnp.zeros((ROWS, LANES), jnp.int32)
     behind = jnp.zeros((ROWS, LANES), jnp.int32)
@@ -228,9 +200,11 @@
     r["behind"][...] = behind
     r["ahead"][...] = ahead
     lane = lax.broadcasted_iota(jnp.int32, (ROWS, LANES), 1)
-    for t in range(pool.shape[0] // LANES):
+    for t in range(N_DP * SLOT // LANES):
         r["chosen"][:, lanes(t)] = (pick == lane + t * LANES).astype(F32).astype(BF)
 
+
+def load_inputs(pool, gain1, r):
     def gather(t, carry):
         cols = pl.ds(pl.multiple_of(t * TILE, TILE), TILE)
         r["unit_in"][:, cols] = dot(r["chosen"][...], pool[:, cols])
@@ -259,9 +233,8 @@
         r["normed_t"][lanes(b), :] = r["normed"][:, lanes(b)].T
 
 
-def project(w, wait_tile, r):
+def project(w, r):
     def tile(t, carry):
-        wait_tile(t)
         cols = pl.ds(pl.multiple_of(t * TILE, TILE), TILE)
         gates = pl.ds(pl.multiple_of(t * TILE + WIDTH, TILE), TILE)
         linear = dot(r["normed"][...], w[:, cols])
@@ -420,7 +393,7 @@
 WORK = (
     ("behind", (ROWS, LANES), jnp.int32),
     ("ahead", (ROWS, LANES), jnp.int32),
-    ("chosen", (ROWS, 640), BF),
+    ("chosen", (ROWS, N_DP * SLOT), BF),
     ("unit_in", (ROWS, WIDTH), F32),
     ("inv_in", (ROWS, LANES), F32),
     ("normed", (ROWS, WIDTH), BF),
@@ -436,29 +409,6 @@
 )
 
 
-def forward(lengths, offsets, pool, w_hbm, gain1, w_depth, gain2, cotangent, output, w, w_sems, r):
-    def copy_w(t, h):
-        cols = pl.ds(pl.multiple_of(t * TILE + h * WIDTH, TILE), TILE)
-        return pltpu.make_async_copy(w_hbm.at[:, cols], w.at[:, cols], w_sems.at[h, t])
-
-    for t in range(WIDTH // TILE):
-        for h in range(2):
-            copy_w(t, h).start()
-
-    def wait_tile(t):
-        for h in range(2):
-            copy_w(t, h).wait()
-
-    for name in ("gated", "conv"):
-        r[name][:, 0:PAD, :] = jnp.zeros((BLOCKS, PAD, LANES), F32)
-        r[name][:, PAD + ROWS :, :] = jnp.zeros((BLOCKS, PAD, LANES), F32)
-    load_inputs(lengths, offsets, pool, gain1, r)
-    project(w, wait_tile, r)
-    convolve(w_depth, r)
-    finish_forward(gain2, cotangent, output, r)
-    transpose_normed(r)
-
-
 def add_blocks(dst, src, count, cols):
     def step(i, carry):
         block, row = i // 2, pl.multiple_of((i % 2) * 48, 48)
@@ -474,9 +424,9 @@
 
 
 def module_kernel(
-    lengths, offsets, pool, w_hbm, gain1, w_depth, gain2, cotangent,
-    output, grad_input, out, small_out,
-    w, w_sems, small, part, rx0, rx1, rx2, rx3, rx3_all, rx4, red, fin, rxs, rxd, small_fin,
+    frames, slot_dest, lengths, offsets, gain1, w_own, w_depth, gain2, cotangent,
+    output, grad_input, out, depth_out, gain1_out, gain2_out,
+    arriving, pool, w, outgoing, own_sem, a2a_send, a2a_recv, w_send, w_recv, small, part, rx0, rx1, rx2, rx3, rx3_all, rx4, red, fin, rxs, rxd, small_fin,
     s0, r0, s1, r1, s2, r2, s3, r3, s4, r4, s5, r5, st1, rt1, st2, rt2, st3, rt3,
     *work
 ):
@@ -676,8 +626,25 @@
             small_fin[:, column(g)] = total
             each(N_SHARD, lambda i: small_final_copy(i).start())
 
-    forward(lengths, offsets, pool, w_hbm, gain1, w_depth, gain2, cotangent, output, w, w_sems, r)
     pl.semaphore_wait(barrier, 30)
+
+    def between():
+        for name in ("gated", "conv"):
+            r[name][:, 0:PAD, :] = jnp.zeros((BLOCKS, PAD, LANES), F32)
+            r[name][:, PAD + ROWS :, :] = jnp.zeros((BLOCKS, PAD, LANES), F32)
+        find_rows(lengths, offsets, r)
+
+    finish_weight, finish_sends = exchange(
+        frames, slot_dest, w_own, arriving, w, outgoing, own_sem, a2a_send, a2a_recv, w_send, w_recv, between
+    )
+    for s in range(N_DP):
+        pool[s * SLOT : (s + 1) * SLOT, :] = arriving[s]
+    load_inputs(pool, gain1, r)
+    finish_weight()
+    project(w, r)
+    convolve(w_depth, r)
+    finish_forward(gain2, cotangent, output, r)
+    transpose_normed(r)
     for k in range(CHUNKS):
         back_convolve(k, w_depth, small, r)
         weight_term(k, part.at[k], r)
@@ -700,9 +667,9 @@
     start_y1(1)
     finish_x(0)
     start_pieces(0)
-    add_small_shard()
     finish_y(2)
     x_copy(2).start()
+    add_small_shard()
     turn_y(1)
     turn_pieces(0)
     finish_x(2)
@@ -712,6 +679,7 @@
     add_small_dp()
     turn_pieces(2)
     turn_pieces(1)
+    finish_pieces(0)
 
     def take_final(j):
         remote(
@@ -719,9 +687,13 @@
         ).wait_recv()
 
     each_owner(take_final)
-    small_out[...] = small_fin[...] * scale
-    for k in (0, 2, 1):
-        finish_pieces(k)
+    depth_out[...] = small_fin[0:TAPS, :] * scale
+    for b in range(BLOCKS):
+        gain1_out[lanes(b)] = small_fin[TAPS, lanes(b)] * scale
+        gain2_out[lanes(b)] = small_fin[TAPS + 1, lanes(b)] * scale
+    finish_sends()
+    finish_pieces(2)
+    finish_pieces(1)
 
     for k in range(CHUNKS):
         core_copy(k).wait_send()
@@ -747,7 +719,7 @@
         each(16, sent)
 
 
-def module(lengths, offsets, pool, full, gain1, w_depth, gain2, cotangent):
+def module(frames, slot_dest, lengths, offsets, gain1, w_in, w_depth, gain2, cotangent):
     vmem = pl.BlockSpec(memory_space=pltpu.VMEM)
     smem = pl.BlockSpec(memory_space=pltpu.SMEM)
     block = WIDTH // N_SHARD
@@ -758,13 +730,20 @@
             jax.ShapeDtypeStruct((ROWS, WIDTH), BF),
             jax.ShapeDtypeStruct((ROWS, WIDTH), BF),
             jax.ShapeDtypeStruct((block, 2 * WIDTH), F32),
-            jax.ShapeDtypeStruct((SMALL_ROWS, WIDTH), F32),
+            jax.ShapeDtypeStruct((TAPS, WIDTH), F32),
+            jax.ShapeDtypeStruct((WIDTH,), F32),
+            jax.ShapeDtypeStruct((WIDTH,), F32),
         ),
-        in_specs=[smem, smem, vmem, pl.BlockSpec(memory_space=pl.ANY), vmem, vmem, vmem, vmem],
-        out_specs=(vmem,) * 4,
+        in_specs=[vmem, smem, smem, smem, vmem, pl.BlockSpec(memory_space=pl.ANY), vmem, vmem, vmem],
+        out_specs=(vmem,) * 6,
         scratch_shapes=[
+            pltpu.VMEM((N_DP, SLOT, WIDTH), BF),
+            pltpu.VMEM((N_DP * SLOT, WIDTH), BF),
             pltpu.VMEM((WIDTH, 2 * WIDTH), BF),
-            dma((2, WIDTH // TILE)),
+            pltpu.VMEM((N_DP, SLOT, WIDTH), BF),
+            dma,
+            dma((N_DP,)), dma((N_DP,)),
+            dma((15,)), dma((15,)),
             pltpu.VMEM((SMALL_ROWS, WIDTH), F32),
             pltpu.VMEM((CHUNKS, 2, 4, 2, block, CHUNK), BF),
             pltpu.VMEM((CHUNKS, 2, 4, block, CHUNK), BF),
@@ -790,21 +769,14 @@
             *[pltpu.VMEM(shape, dtype) for _, shape, dtype in WORK],
         ],
         compiler_params=pltpu.CompilerParams(
-            collective_id=1, has_side_effects=True, vmem_limit_bytes=60 * 1024 * 1024
+            collective_id=0, has_side_effects=True, vmem_limit_bytes=64 * 1024 * 1024 - 65536
         ),
         name="module",
-    )(lengths, offsets, pool, full, gain1, w_depth, gain2, cotangent)
+    )(frames, slot_dest, lengths, offsets, gain1, w_in, w_depth, gain2, cotangent)
 
 
 def body(frames, slot_dest, recv_length, recv_offset, gain1, w_in, w_depth, gain2, cotangent):
-    model_width = frames.shape[2]
-    taps = w_depth.shape[0]
-    pool, full = exchange(frames, slot_dest, w_in)
-    output, grad_input, grad_w, small_sum = module(
-        recv_length, recv_offset, pool.reshape(-1, model_width), full.reshape(model_width, 2 * model_width),
-        gain1, w_depth, gain2, cotangent,
-    )
-    return (output, grad_input, grad_w, small_sum[:taps], small_sum[taps], small_sum[taps + 1])
+    return module(frames, slot_dest, recv_length, recv_offset, gain1, w_in, w_depth, gain2, cotangent)
 
 
 def solution(mesh):

time: 211 us -> 188 us (0.89)
  Pallas kernels: 194 us -> 179 us
  local copies, waits for them, and re-layouts: 16.4 us -> 7.12 us
    pallas_call x1 -> x0, Pallas kernels: 63.2 us -> none  [exchange(): pl.pallas_call(exchange_kernel, out_shape=(jax.ShapeDtypeStruct((slots, s...]
    pallas_call x1, Pallas kernels: 131 us -> 179 us  [module(): pl.pallas_call(module_kernel, out_shape=(jax.ShapeDtypeStruct((ROWS, WIDT...]
    unnamed x17 -> x16, local copies, waits for them, and re-layouts: 13.3 us -> 7.12 us
    slice x2 -> x0, local copies, waits for them, and re-layouts: 3.07 us -> none  [the longest x1 1.62 us: body(): small_sum[:taps]]
where the time goes in v4:
time: 188 us; the launch traced here: 187 us
  Pallas kernels  179 us (95%)
  local copies, waits for them, and re-layouts  7.12 us (4%)
    pallas_call x1, Pallas kernels, module(): pl.pallas_call(module_kernel, out_shape=(jax.ShapeDtypeStruct((ROWS, WIDT...  179 us
    unnamed x16, local copies, waits for them, and re-layouts  7.12 us

profile of v4, /device:TPU:6, one launch (start us, length us, event | category | flops | bytes accessed | tf_op | source)
XLA Modules:
  0.0 187.0 jit_solution(12451307595071982468)
XLA Ops:
  0.6 179.2 %module.1 = (bf16[384,1536]{1,0:T(8,128)(2,1)}, bf16[384,1536]{1,0:T(8,128)(2,1)}, f32[96,3072]{1,0:T(8,128)}, f32[31,1536]{1,0:T(8,128)}, f32[1536]{0:T(1024)}, /*index=5*/f32[1536]{0:T(1024)}) custom-call(bf16[16,40,1536]{2,1,0:T(8,128)(2,1)} %frames.1, s32[16]{0:T(128)} %slot_dest.1, s32[16]{0:T(128)} %lengths.1, s32[16]{0:T(128)} %offsets.1, ...), custom_call_target="tpu_custom_call" | custom-call | tf_op jit(solution)/shard_map/module/pallas_call | solution.py:727
  179.9 0.0 copy-start.1
  179.9 2.5 %copy.21 = bf16[384,1536]{1,0:T(8,128)(2,1)} copy(bf16[384,1536]{1,0:T(8,128)(2,1)} %get-tuple-element.12) | data formatting | bytes 2359296
  182.3 0.0 copy-done.1
  182.3 0.0 copy-start
  182.3 1.0 copy.22
  183.4 0.7 copy-done
  184.0 0.0 copy-start.2
  184.0 0.0 copy-start.4
  184.0 0.0 copy-start.3
  184.0 1.0 copy.23
  185.1 0.1 copy-done.2
  185.1 0.7 copy.24
  185.8 0.0 copy-done.4
  185.8 0.6 copy.25
  186.4 0.0 copy-done.3
  186.4 0.6 copy.26
Async XLA Ops:
  179.9 2.5 %copy-start.1 = (bf16[384,1536]{1,0:T(8,128)(2,1)S(1)}, bf16[384,1536]{1,0:T(8,128)(2,1)}, u32[]{:S(2)}) copy-start(bf16[384,1536]{1,0:T(8,128)(2,1)} %get-tuple-element.13) | copy-start | bytes 3538948
  182.3 1.7 copy-start
  184.0 1.1 copy-start.2
  184.0 1.8 copy-start.4
  184.0 2.4 %copy-start.3 = (f32[1536]{0:T(1024)S(1)}, f32[1536]{0:T(1024)}, u32[]{:S(2)}) copy-start(f32[1536]{0:T(1024)} %get-tuple-element.17) | copy-start | bytes 18436

commit v5 on v4

--- a/solution.py
+++ b/solution.py
@@ -40,7 +40,7 @@
     return jnp.minimum(index, N_DP - 1)
 
 
-def exchange(frames, slot_dest, w_own, pool, w, outgoing, own_sem, a2a_send, a2a_recv, w_send, w_recv, between):
+def exchange(frames, slot_dest, w_own, pool, w, outgoing, own_sem, a2a_send, a2a_recv, w_send, w_recv, ready, between):
     p, g = lax.axis_index("dp"), lax.axis_index("shard")
     x_lo, y, core = g // 8, (g // 2) % 4, g % 2
     up, down, across = (y + 1) % 4, (y + 3) % 4, (y + 2) % 4
@@ -50,6 +50,14 @@
     g_core = shard_index(x_lo, y, 1 - core)
     depth = w_own.shape[0]
 
+    def order(j, carry):
+        outgoing[j] = frames[source_of(slot_dest, (p + j) % N_DP)]
+        return carry
+
+    lax.fori_loop(1, N_DP, order, 0)
+    pool[p] = frames[source_of(slot_dest, p)]
+    ready()
+
     def rows(block):
         return w.at[pl.ds(pl.multiple_of(block * depth, depth), depth), :]
 
@@ -68,27 +76,31 @@
     go(send(g, g_down, 2, w_own))
     go(send(g, g_x, 0, w_own))
 
-    def post(i, carry):
-        d = (p + i + 6) % N_DP
-        j = jnp.where(i + 6 < N_DP, i + 6, i + 6 - N_DP)
-        outgoing[j] = frames[source_of(slot_dest, d)]
+    def post(j):
+        d = (p + j) % N_DP
         remote(outgoing.at[j], pool.at[p], a2a_send.at[j], a2a_recv.at[j], (d, g)).start()
-        return carry
-
-    lax.fori_loop(0, N_DP - 6, post, 0)
-    lax.fori_loop(N_DP - 5, N_DP, post, 0)
+
+    def post_even(i, carry):
+        post(2 * i)
+        return carry
+
+    def post_odd(i, carry):
+        post(2 * i + 1)
+        return carry
+
+    lax.fori_loop(1, N_DP // 2, post_even, 0)
+    lax.fori_loop(0, N_DP // 2, post_odd, 0)
     go(send(g, g_core, 7, w_own))
     own_w = pltpu.make_async_copy(w_own, rows(g), own_sem)
     own_w.start()
-    pool[p] = frames[source_of(slot_dest, p)]
     between()
 
     def arrived(block, slot):
         remote(rows(block), rows(block), w_send.at[slot], w_recv.at[slot], (p, g_x)).wait_recv()
 
     arrived(g_x, 0)
+    go(send(g_x, g_down, 4))
     go(send(g_x, g_up, 3))
-    go(send(g_x, g_down, 4))
     go(send(g_x, g_core, 8))
     b = shard_index(x_lo, down, core)
     arrived(b, 1)
@@ -233,47 +245,51 @@
         r["normed_t"][lanes(b), :] = r["normed"][:, lanes(b)].T
 
 
-def project(w, r):
-    def tile(t, carry):
-        cols = pl.ds(pl.multiple_of(t * TILE, TILE), TILE)
-        gates = pl.ds(pl.multiple_of(t * TILE + WIDTH, TILE), TILE)
-        linear = dot(r["normed"][...], w[:, cols])
-        sig = sigmoid(dot(r["normed"][...], w[:, gates]))
-        r["linear"][:, cols] = linear
-        r["sig"][:, cols] = sig
-        gated = (linear * sig).astype(BF).astype(F32)
-        for j in range(TILE // LANES):
-            r["gated"][t * (TILE // LANES) + j, PAD : PAD + ROWS, :] = gated[:, j * LANES : (j + 1) * LANES]
-        return carry
-
-    lax.fori_loop(0, WIDTH // TILE, tile, 0)
+def project_tile(t, w, r):
+    cols = pl.ds(pl.multiple_of(t * TILE, TILE), TILE)
+    gates = pl.ds(pl.multiple_of(t * TILE + WIDTH, TILE), TILE)
+    linear = dot(r["normed"][...], w[:, cols])
+    sig = sigmoid(dot(r["normed"][...], w[:, gates]))
+    r["linear"][:, cols] = linear
+    r["sig"][:, cols] = sig
+    gated = (linear * sig).astype(BF).astype(F32)
+    for j in range(TILE // LANES):
+        r["gated"][t * (TILE // LANES) + j, PAD : PAD + ROWS, :] = gated[:, j * LANES : (j + 1) * LANES]
 
 
 def tap_mask(behind, ahead, shift):
     return ahead >= shift if shift > 0 else behind >= -shift
 
 
-def convolve(w_depth, r):
-    def pair(c, carry):
-        for g in range(ROWS // GROUP):
-            begin = g * GROUP
-            behind = r["behind"][begin : begin + GROUP, :]
-            ahead = r["ahead"][begin : begin + GROUP, :]
-            total = [jnp.zeros((GROUP, LANES), F32)] * 2
-            for k in range(TAPS):
-                shift = k - REACH
-                same = tap_mask(behind, ahead, shift)
-                for j in range(2):
-                    b = c * 2 + j
-                    x = r["gated"][b, PAD + begin + shift : PAD + begin + shift + GROUP, :]
-                    if shift != 0:
-                        x = jnp.where(same, x, 0.0)
-                    total[j] = total[j] + x * w_depth[k : k + 1, lanes(b)]
+def convolve_pair(c, w_depth, r):
+    for g in range(ROWS // GROUP):
+        begin = g * GROUP
+        behind = r["behind"][begin : begin + GROUP, :]
+        ahead = r["ahead"][begin : begin + GROUP, :]
+        total = [jnp.zeros((GROUP, LANES), F32)] * 2
+        for k in range(TAPS):
+            shift = k - REACH
+            same = tap_mask(behind, ahead, shift)
             for j in range(2):
-                r["conv"][c * 2 + j, PAD + begin : PAD + begin + GROUP, :] = total[j]
-        return carry
-
-    lax.fori_loop(0, BLOCKS // 2, pair, 0)
+                b = c * 2 + j
+                x = r["gated"][b, PAD + begin + shift : PAD + begin + shift + GROUP, :]
+                if shift != 0:
+                    x = jnp.where(same, x, 0.0)
+                total[j] = total[j] + x * w_depth[k : k + 1, lanes(b)]
+        for j in range(2):
+            r["conv"][c * 2 + j, PAD + begin : PAD + begin + GROUP, :] = total[j]
+
+
+def project_and_convolve(w, w_depth, r):
+    project_tile(0, w, r)
+
+    def step(t, carry):
+        convolve_pair(t - 1, w_depth, r)
+        project_tile(t, w, r)
+        return carry
+
+    lax.fori_loop(1, BLOCKS // 2, step, 0)
+    convolve_pair(BLOCKS // 2 - 1, w_depth, r)
 
 
 def finish_forward(gain2, cotangent, output, r):
@@ -307,47 +323,54 @@
     lax.fori_loop(0, ROWS // STEP, row_step, 0)
 
 
-def back_convolve(chunk, w_depth, small, r):
-    def pair(c, carry):
-        first = chunk * (HALF // LANES) + c * 2
-        r["tap_sum"][...] = jnp.zeros_like(r["tap_sum"])
-        for g in range(ROWS // GROUP):
-            begin = g * GROUP
-            rows = slice(begin, begin + GROUP)
-            behind = r["behind"][rows, :]
-            ahead = r["ahead"][rows, :]
-            total = [jnp.zeros((GROUP, LANES), F32)] * 2
-            gated = [r["gated"][first + j, PAD + begin : PAD + begin + GROUP, :] for j in range(2)]
-            for k in range(TAPS):
-                shift = REACH - k
-                same = tap_mask(behind, ahead, shift)
-                for j in range(2):
-                    x = r["conv"][first + j, PAD + begin + shift : PAD + begin + shift + GROUP, :]
-                    if shift != 0:
-                        x = jnp.where(same, x, 0.0)
-                    total[j] = total[j] + x * w_depth[k : k + 1, lanes(first + j)]
-                    product = x * gated[j]
-                    r["tap_sum"][j, k] = r["tap_sum"][j, k] + fold(product)
+def back_convolve_pair(c, w_depth, small, r):
+    first = c * 2
+    r["tap_sum"][...] = jnp.zeros_like(r["tap_sum"])
+    for g in range(ROWS // GROUP):
+        begin = g * GROUP
+        rows = slice(begin, begin + GROUP)
+        behind = r["behind"][rows, :]
+        ahead = r["ahead"][rows, :]
+        total = [jnp.zeros((GROUP, LANES), F32)] * 2
+        gated = [r["gated"][first + j, PAD + begin : PAD + begin + GROUP, :] for j in range(2)]
+        for k in range(TAPS):
+            shift = REACH - k
+            same = tap_mask(behind, ahead, shift)
             for j in range(2):
-                at = pl.multiple_of((first + j) * LANES, LANES)
-                linear = r["linear"][rows, pl.ds(at, LANES)]
-                sig = r["sig"][rows, pl.ds(at, LANES)]
-                grad = total[j] * sig
-                r["grad_pre"][rows, pl.ds(at, LANES)] = grad.astype(BF)
-                r["grad_pre"][rows, pl.ds(at + WIDTH, LANES)] = (grad * linear * (1.0 - sig)).astype(BF)
+                x = r["conv"][first + j, PAD + begin + shift : PAD + begin + shift + GROUP, :]
+                if shift != 0:
+                    x = jnp.where(same, x, 0.0)
+                total[j] = total[j] + x * w_depth[k : k + 1, lanes(first + j)]
+                product = x * gated[j]
+                r["tap_sum"][j, k] = r["tap_sum"][j, k] + fold(product)
         for j in range(2):
             at = pl.multiple_of((first + j) * LANES, LANES)
-            small[0:TAPS, pl.ds(at, LANES)] = jnp.sum(r["tap_sum"][j], axis=1)
-        return carry
-
-    lax.fori_loop(0, HALF // LANES // 2, pair, 0)
+            linear = r["linear"][rows, pl.ds(at, LANES)]
+            sig = r["sig"][rows, pl.ds(at, LANES)]
+            grad = total[j] * sig
+            r["grad_pre"][rows, pl.ds(at, LANES)] = grad.astype(BF)
+            r["grad_pre"][rows, pl.ds(at + WIDTH, LANES)] = (grad * linear * (1.0 - sig)).astype(BF)
+    for j in range(2):
+        at = pl.multiple_of((first + j) * LANES, LANES)
+        small[0:TAPS, pl.ds(at, LANES)] = jnp.sum(r["tap_sum"][j], axis=1)
+
+
+def back_convolve(chunk, w_depth, small, r, beside):
+    count = HALF // LANES // 2
+
+    def pair(c, carry):
+        back_convolve_pair(chunk * count + c, w_depth, small, r)
+        beside(c)
+        return carry
+
+    lax.fori_loop(0, count, pair, 0)
 
 
 def weight_term(chunk, part, r):
     def tile(i, carry):
         rows = pl.ds(pl.multiple_of(i * 384, 384), 384)
         for h in range(2):
-            cols = pl.ds(h * WIDTH + chunk * HALF, HALF)
+            cols = pl.ds(pl.multiple_of(h * WIDTH + chunk * HALF, HALF), HALF)
             value = dot(r["normed_t"][rows, :], r["grad_pre"][:, cols]).astype(BF)
             for q in range(4):
                 part[i // 2, (i % 2) * 2 + q // 2, q % 2, :, h * HALF : (h + 1) * HALF] = value[q * 96 : (q + 1) * 96]
@@ -356,10 +379,11 @@
     lax.fori_loop(0, 4, tile, 0)
 
 
-def back_project(w, r):
+def back_project(w, r, beside):
     def tile(t, carry):
         cols = pl.ds(pl.multiple_of(t * TILE, TILE), TILE)
         r["linear"][:, cols] = dot_t(r["grad_pre"][...], w[cols, :])
+        beside(t)
         return carry
 
     lax.fori_loop(0, WIDTH // TILE, tile, 0)
@@ -424,9 +448,9 @@
 
 
 def module_kernel(
-    frames, slot_dest, lengths, offsets, gain1, w_own, w_depth, gain2, cotangent,
-    output, grad_input, out, depth_out, gain1_out, gain2_out,
-    arriving, pool, w, outgoing, own_sem, a2a_send, a2a_recv, w_send, w_recv, small, part, rx0, rx1, rx2, rx3, rx3_all, rx4, red, fin, rxs, rxd, small_fin,
+    frames_hbm, slot_dest, lengths, offsets, gain1, w_own, w_depth, gain2, cotangent_hbm,
+    output_hbm, grad_input_hbm, out, depth_out, gain1_out, gain2_out,
+    frames, cotangent, output, grad_input, io_sems, arriving, pool, w, outgoing, own_sem, a2a_send, a2a_recv, w_send, w_recv, small, part, rx0, rx1, rx2, rx3, rx3_all, rx4, red, fin, rxs, rxd, small_fin,
     s0, r0, s1, r1, s2, r2, s3, r3, s4, r4, s5, r5, st1, rt1, st2, rt2, st3, rt3,
     *work
 ):
@@ -626,7 +650,16 @@
             small_fin[:, column(g)] = total
             each(N_SHARD, lambda i: small_final_copy(i).start())
 
-    pl.semaphore_wait(barrier, 30)
+    load_frames = pltpu.make_async_copy(frames_hbm, frames, io_sems.at[0])
+    load_frames.start()
+    load_cotangent = pltpu.make_async_copy(cotangent_hbm, cotangent, io_sems.at[1])
+    load_cotangent.start()
+    store_output = pltpu.make_async_copy(output, output_hbm, io_sems.at[2])
+    store_grad = pltpu.make_async_copy(grad_input, grad_input_hbm, io_sems.at[3])
+    load_frames.wait()
+
+    def ready():
+        pl.semaphore_wait(barrier, 30)
 
     def between():
         for name in ("gated", "conv"):
@@ -635,43 +668,63 @@
         find_rows(lengths, offsets, r)
 
     finish_weight, finish_sends = exchange(
-        frames, slot_dest, w_own, arriving, w, outgoing, own_sem, a2a_send, a2a_recv, w_send, w_recv, between
+        frames, slot_dest, w_own, arriving, w, outgoing, own_sem, a2a_send, a2a_recv, w_send, w_recv, ready, between
     )
     for s in range(N_DP):
         pool[s * SLOT : (s + 1) * SLOT, :] = arriving[s]
     load_inputs(pool, gain1, r)
     finish_weight()
-    project(w, r)
-    convolve(w_depth, r)
+    project_and_convolve(w, w_depth, r)
+    load_cotangent.wait()
     finish_forward(gain2, cotangent, output, r)
+    store_output.start()
     transpose_normed(r)
-    for k in range(CHUNKS):
-        back_convolve(k, w_depth, small, r)
+    def beside_first(c):
+        pass
+
+    def beside_second(c):
+        @pl.when(c == 0)
+        def _():
+            finish_core(0)
+            start_y1(0)
+
+    def beside_third(c):
+        @pl.when(c == 0)
+        def _():
+            finish_core(1)
+            x_copy(1).start()
+            turn_y(0)
+
+    for k, beside in enumerate((beside_first, beside_second, beside_third)):
+        back_convolve(k, w_depth, small, r, beside)
         weight_term(k, part.at[k], r)
         core_copy(k).start()
-        if k == 1:
-            finish_core(0)
-            start_y1(0)
-    finish_core(1)
-    x_copy(1).start()
-    back_project(w, r)
-    finish_core(2)
-    start_y1(2)
-    turn_y(0)
-    finish_back(gain1, grad_input, small, r)
-    each_owner(lambda j: small_copy(j).start())
     finish_y(0)
     x_copy(0).start()
+
+    def beside(t):
+        @pl.when(t == 2)
+        def _():
+            finish_core(2)
+            start_y1(2)
+
+        @pl.when(t == 5)
+        def _():
+            finish_x(0)
+            start_pieces(0)
+
+    back_project(w, r, beside)
+    finish_back(gain1, grad_input, small, r)
+    store_grad.start()
+    each_owner(lambda j: small_copy(j).start())
     turn_y(2)
     finish_x(1)
     start_y1(1)
-    finish_x(0)
-    start_pieces(0)
+    turn_pieces(0)
     finish_y(2)
     x_copy(2).start()
     add_small_shard()
     turn_y(1)
-    turn_pieces(0)
     finish_x(2)
     start_pieces(2)
     finish_y(1)
@@ -692,6 +745,8 @@
         gain1_out[lanes(b)] = small_fin[TAPS, lanes(b)] * scale
         gain2_out[lanes(b)] = small_fin[TAPS + 1, lanes(b)] * scale
     finish_sends()
+    store_output.wait()
+    store_grad.wait()
     finish_pieces(2)
     finish_pieces(1)
 
@@ -722,6 +777,7 @@
 def module(frames, slot_dest, lengths, offsets, gain1, w_in, w_depth, gain2, cotangent):
     vmem = pl.BlockSpec(memory_space=pltpu.VMEM)
     smem = pl.BlockSpec(memory_space=pltpu.SMEM)
+    hbm = pl.BlockSpec(memory_space=pl.ANY)
     block = WIDTH // N_SHARD
     dma = pltpu.SemaphoreType.DMA
     return pl.pallas_call(
@@ -734,9 +790,14 @@
             jax.ShapeDtypeStruct((WIDTH,), F32),
             jax.ShapeDtypeStruct((WIDTH,), F32),
         ),
-        in_specs=[vmem, smem, smem, smem, vmem, pl.BlockSpec(memory_space=pl.ANY), vmem, vmem, vmem],
-        out_specs=(vmem,) * 6,
+        in_specs=[hbm, smem, smem, smem, vmem, hbm, vmem, vmem, hbm],
+        out_specs=(hbm, hbm, vmem, vmem, vmem, vmem),
         scratch_shapes=[
+            pltpu.VMEM((N_DP, SLOT, WIDTH), BF),
+            pltpu.VMEM((ROWS, WIDTH), BF),
+            pltpu.VMEM((ROWS, WIDTH), BF),
+            pltpu.VMEM((ROWS, WIDTH), BF),
+            dma((4,)),
             pltpu.VMEM((N_DP, SLOT, WIDTH), BF),
             pltpu.VMEM((N_DP * SLOT, WIDTH), BF),
             pltpu.VMEM((WIDTH, 2 * WIDTH), BF),

time: 188 us -> 177 us (0.941)
  Pallas kernels: 179 us -> 168 us
    pallas_call x1, Pallas kernels: 179 us -> 168 us  [module(): pl.pallas_call(module_kernel, out_shape=(jax.ShapeDtypeStruct((ROWS, WIDT...]
where the time goes in v5:
time: 177 us; the launch traced here: 176 us
  Pallas kernels  168 us (95%)
  local copies, waits for them, and re-layouts  7.12 us (4%)
    pallas_call x1, Pallas kernels, module(): pl.pallas_call(module_kernel, out_shape=(jax.ShapeDtypeStruct((ROWS, WIDT...  168 us
    unnamed x16, local copies, waits for them, and re-layouts  7.12 us

profile of v5, /device:TPU:6, one launch (start us, length us, event | category | flops | bytes accessed | tf_op | source)
XLA Modules:
  0.0 175.8 jit_solution(17874088655684966616)
XLA Ops:
  0.6 168.0 %module.1 = (bf16[384,1536]{1,0:T(8,128)(2,1)}, bf16[384,1536]{1,0:T(8,128)(2,1)}, f32[96,3072]{1,0:T(8,128)}, f32[31,1536]{1,0:T(8,128)}, f32[1536]{0:T(1024)}, /*index=5*/f32[1536]{0:T(1024)}) custom-call(bf16[16,40,1536]{2,1,0:T(8,128)(2,1)} %frames_hbm.1, s32[16]{0:T(128)} %slot_dest.1, s32[16]{0:T(128)} %lengths.1, s32[16]{0:T(128)} %offsets.1, ...), custom_call_target="tpu_custom_call" | custom-call | tf_op jit(solution)/shard_map/module/pallas_call | solution.py:783
  168.7 0.0 copy-start.1
  168.7 2.5 %copy.21 = bf16[384,1536]{1,0:T(8,128)(2,1)} copy(bf16[384,1536]{1,0:T(8,128)(2,1)} %get-tuple-element.12) | data formatting | bytes 2359296
  171.1 0.0 copy-done.1
  171.1 0.0 copy-start
  171.1 1.0 copy.22
  172.2 0.7 copy-done
  172.8 0.0 copy-start.2
  172.8 0.0 copy-start.4
  172.8 0.0 copy-start.3
  172.8 1.0 copy.23
  173.9 0.1 copy-done.2
  173.9 0.7 copy.24
  174.6 0.0 copy-done.4
  174.6 0.6 copy.25
  175.2 0.0 copy-done.3
  175.2 0.6 copy.26
Async XLA Ops:
  168.7 2.5 %copy-start.1 = (bf16[384,1536]{1,0:T(8,128)(2,1)S(1)}, bf16[384,1536]{1,0:T(8,128)(2,1)}, u32[]{:S(2)}) copy-start(bf16[384,1536]{1,0:T(8,128)(2,1)} %get-tuple-element.13) | copy-start | bytes 3538948
  171.1 1.7 copy-start
  172.8 1.1 copy-start.2
  172.8 1.8 %copy-start.4 = (f32[1536]{0:T(1024)S(1)}, f32[1536]{0:T(1024)}, u32[]{:S(2)}) copy-start(f32[1536]{0:T(1024)} %get-tuple-element.16) | copy-start | bytes 18436
  172.8 2.4 %copy-start.3 = (f32[1536]{0:T(1024)S(1)}, f32[1536]{0:T(1024)}, u32[]{:S(2)}) copy-start(f32[1536]{0:T(1024)} %get-tuple-element.17) | copy-start | bytes 18436

commit v6 on v5

--- a/solution.py
+++ b/solution.py
@@ -437,8 +437,7 @@
     def step(i, carry):
         block, row = i // 2, pl.multiple_of((i % 2) * 48, 48)
         d, s = dst(block), src(block)
-        value = d[pl.ds(row, 48), cols].astype(F32) + s[pl.ds(row, 48), :].astype(F32)
-        d[pl.ds(row, 48), cols] = value.astype(BF)
+        d[pl.ds(row, 48), cols] = d[pl.ds(row, 48), cols] + s[pl.ds(row, 48), :]
         return carry
 
     lax.fori_loop(0, count * 2, step, 0)

time: 177 us -> 176 us (level)
  no operation moved by 1% of the time
where the time goes in v6:
time: 176 us; the launch traced here: 175 us
  Pallas kernels  168 us (95%)
  local copies, waits for them, and re-layouts  7.12 us (4%)
    pallas_call x1, Pallas kernels, module(): pl.pallas_call(module_kernel, out_shape=(jax.ShapeDtypeStruct((ROWS, WIDT...  168 us
    unnamed x16, local copies, waits for them, and re-layouts  7.12 us

profile of v6, /device:TPU:6, one launch (start us, length us, event | category | flops | bytes accessed | tf_op | source)
XLA Modules:
  0.0 175.4 jit_solution(10197907978034982025)
XLA Ops:
  0.6 167.6 %module.1 = (bf16[384,1536]{1,0:T(8,128)(2,1)}, bf16[384,1536]{1,0:T(8,128)(2,1)}, f32[96,3072]{1,0:T(8,128)}, f32[31,1536]{1,0:T(8,128)}, f32[1536]{0:T(1024)}, /*index=5*/f32[1536]{0:T(1024)}) custom-call(bf16[16,40,1536]{2,1,0:T(8,128)(2,1)} %frames_hbm.1, s32[16]{0:T(128)} %slot_dest.1, s32[16]{0:T(128)} %lengths.1, s32[16]{0:T(128)} %offsets.1, ...), custom_call_target="tpu_custom_call" | custom-call | tf_op jit(solution)/shard_map/module/pallas_call | solution.py:782
  168.2 0.0 copy-start.1
  168.3 2.5 %copy.21 = bf16[384,1536]{1,0:T(8,128)(2,1)} copy(bf16[384,1536]{1,0:T(8,128)(2,1)} %get-tuple-element.12) | data formatting | bytes 2359296
  170.7 0.0 copy-done.1
  170.7 0.0 copy-start
  170.7 1.0 copy.22
  171.7 0.7 copy-done
  172.4 0.0 copy-start.2
  172.4 0.0 copy-start.4
  172.4 0.0 copy-start.3
  172.4 1.0 copy.23
  173.4 0.1 copy-done.2
  173.5 0.7 copy.24
  174.2 0.0 copy-done.4
  174.2 0.6 copy.25
  174.8 0.0 copy-done.3
  174.8 0.6 copy.26
Async XLA Ops:
  168.2 2.5 %copy-start.1 = (bf16[384,1536]{1,0:T(8,128)(2,1)S(1)}, bf16[384,1536]{1,0:T(8,128)(2,1)}, u32[]{:S(2)}) copy-start(bf16[384,1536]{1,0:T(8,128)(2,1)} %get-tuple-element.13) | copy-start | bytes 3538948
  170.7 1.7 copy-start
  172.4 1.1 copy-start.2
  172.4 1.8 %copy-start.4 = (f32[1536]{0:T(1024)S(1)}, f32[1536]{0:T(1024)}, u32[]{:S(2)}) copy-start(f32[1536]{0:T(1024)} %get-tuple-element.16) | copy-start | bytes 18436
  172.4 2.4 %copy-start.3 = (f32[1536]{0:T(1024)S(1)}, f32[1536]{0:T(1024)}, u32[]{:S(2)}) copy-start(f32[1536]{0:T(1024)} %get-tuple-element.17) | copy-start | bytes 18436
